TPU v7x, 256 devices: a whole 4x4x8 slice. The times are simulated.
256 devices in a mesh: row: 8 (over y, x_hi), col: 32 (over z, x_lo, core).
Axes of the slice: x: 4 (x_hi: 2, x_lo: 2; x = x_hi * 2 + x_lo), y: 4, z: 8, core: 2. Of those that a mesh axis runs over, the one named last changes fastest.
Arguments:
- inverses: bfloat16 [8, 128, 1024, 1024], P('row', 'col'), as said below
- coupling: bfloat16 [8, 128, 1024, 256], P('row', 'col'), may hold values from -0.1875 to 0.1875
- orders: int32 [8, 128], P('row', 'col'), may hold values from 512 to 1024, as said below
- owners: int32 [8, 128, 1], P(None, 'col'), may hold values from 0 to 7, as said below
- offsets: int32 [8, 128, 2], P(None, 'col'), may hold values from 0 to 2
- dense_slab: float32 [4096, 16384], P('row', 'col'), may hold values from -6 to 6
- pivots: float32 [1024], replicated, may hold values from 16 to 128
Outputs:
- result: float32 [4096, 16384], P('row', 'col')
Inputs may be any that keep to these rules, and one draw needn't show every extreme that they name: `orders`: order of each subdomain; some subdomain has exactly 1024. `owners`: within the 4 subdomains of one device (entries r, s with the same r and the same s // 4) no row block is named twice. `inverses`: each inverse is symmetric.
All inputs are finite; a program needn't handle non-finite values.
Results may differ from a plain program's by a relative error of at most 0.0035.
Values may be sent and summed in bfloat16 or wider, within the bound.
No kernel may reach another device: no remote copies, remote signals or barrier semaphores. Data moves between devices by JAX's collectives and lax.ppermute only.
A program may use at most 64 MiB of HBM per device.

v0:
```python
import jax
import jax.numpy as jnp
from jax import lax
from jax.sharding import PartitionSpec as P


def spread(value, axis, source):
    kept = jnp.where(lax.axis_index(axis) == source, value, 0).astype(value.dtype)
    return lax.psum(kept, axis)


def place_tile(schur_sum, tile_value, weight, row_start, col_start):
    couple_width = tile_value.shape[0]
    current = lax.dynamic_slice(schur_sum, (row_start, col_start), (couple_width, couple_width))
    return lax.dynamic_update_slice(
        schur_sum, current + weight * tile_value.astype(jnp.float32), (row_start, col_start)
    )


def body(inverses, coupling, orders, owners, offsets, dense_slab, pivots):
    order_size = inverses.shape[2]
    couple_width = coupling.shape[3]
    tile_size = dense_slab.shape[0]
    panel_width = pivots.shape[0]
    offset_unit = (tile_size - couple_width) // 2
    live_rows = jnp.arange(order_size, dtype=jnp.int32)[None, :, None] < orders[0][:, None, None]
    masked = jnp.where(live_rows, coupling[0], jnp.zeros_like(coupling[0]))
    solved = jnp.einsum(
        "sij,sjk->sik", inverses[0], masked, preferred_element_type=jnp.float32
    ).astype(jnp.bfloat16)
    schur_tiles = jnp.einsum(
        "sji,sjk->sik", masked, solved, preferred_element_type=jnp.float32
    ).astype(jnp.bfloat16)
    my_row = lax.axis_index("row")
    targets = owners[:, :, 0].reshape(-1)
    row_starts = offsets[:, :, 0].reshape(-1) * offset_unit
    col_starts = offsets[:, :, 1].reshape(-1) * offset_unit
    zero_sum = jnp.zeros((tile_size, tile_size), jnp.float32)
    shard_tiles = lax.all_gather(schur_tiles, "row", axis=0, tiled=True)

    def one_tile(position, running):
        weight = (targets[position] == my_row).astype(jnp.float32)
        return place_tile(
            running, shard_tiles[position], weight, row_starts[position], col_starts[position]
        )

    schur_sum = lax.fori_loop(0, shard_tiles.shape[0], one_tile, zero_sum)
    updated = dense_slab - schur_sum
    rounded = updated.astype(jnp.bfloat16)
    panel_parts = []
    for part_index in range(panel_width // tile_size):
        panel_parts.append(spread(rounded, "row", part_index))
    panel_cols = jnp.concatenate(panel_parts, axis=0)
    crossed = spread(panel_cols, "col", lax.axis_index("row"))
    left_factor = (crossed.astype(jnp.float32) / pivots[:, None]).astype(jnp.bfloat16)
    update = lax.dot_general(
        left_factor, panel_cols, (((0,), (0,)), ((), ())), preferred_element_type=jnp.float32
    )
    return updated - update


def solution(mesh):
    placed = (
        P("row", "col", None, None),
        P("row", "col", None, None),
        P("row", "col"),
        P(None, "col", None),
        P(None, "col", None),
        P("row", "col"),
        P(),
    )
    return jax.shard_map(
        body, mesh=mesh, in_specs=placed, out_specs=P("row", "col"), check_vma=False
    )
```

profile of v0, /device:TPU:1, one launch (start us, length us, event | category | flops | bytes accessed | tf_op | source)
XLA Modules:
  0.0 776.2 jit_solution(6413494720437426989)
XLA Ops:
  7.3 8.2 %fusion.8 = bf16[4,256,256]{2,1,0:T(8,128)(2,1)} fusion(bf16[1,4,1024,1024]{3,2,1,0:T(8,128)(2,1)} %param.9, bf16[1,4,1024,256]{3,2,1,0:T(8,128)(2,1)} %param.10, pred[4,1024]{1,0:T(4,128)(4,1)S(1)} %iota_compare_fusion), kind=kOutput, calls=%fused_computation.8 | convolution fusion | flops 2687762432 | bytes 11014144 | tf_op jit(solution)/shard_map/sji,sjk->sik/dot_general | solution.py:31
  16.1 79.4 %all-gather.2.cloned.1.call-done = bf16[32,256,256]{2,1,0:T(8,128)(2,1)} async-done(((bf16[4,256,256]{2,1,0:T(8,128)(2,1)}), bf16[32,256,256]{2,1,0:T(8,128)(2,1)}) %all-gather.2.cloned.1.call-update) | async-done | bytes 4194320 | tf_op jit(solution)/shard_map/all_gather | solution.py:39
  95.6 344.7 %while.13 = (s32[]{:T(128)}, f32[512,512]{1,0:T(8,128)S(1)}, s32[32]{0:T(128)S(1)}, s32[32]{0:T(128)S(1)}, s32[32]{0:T(128)S(1)}, /*index=5*/s32[]{:T(128)}, bf1...) while((s32[]{:T(128)}, f32[512,512]{1,0:T(8,128)S(1)}, s32[32]{0:T(128)S(1)}, s32[32]{0:T(128)S(1)}, ...), condition=%wide.region_1.2_spmd, body=%wide.region_0.1_spmd.sunk | while | flops 196618 | bytes 1179887 | solution.py:47
  103.0 3.3 dynamic_update_slice.8
  113.7 3.9 dynamic_update_slice.8
  124.9 3.9 dynamic_update_slice.8
  136.2 3.9 dynamic_update_slice.8
  147.5 4.7 dynamic_update_slice.8
  179.5 4.7 dynamic_update_slice.8
  201.0 4.7 dynamic_update_slice.8
  213.1 3.9 dynamic_update_slice.8
  234.3 3.9 dynamic_update_slice.8
  255.6 4.7 dynamic_update_slice.8
  277.6 3.9 dynamic_update_slice.8
  318.2 4.7 dynamic_update_slice.8
  340.7 3.3 dynamic_update_slice.8
  381.6 3.9 dynamic_update_slice.8
  392.9 4.7 dynamic_update_slice.8
  405.0 3.3 dynamic_update_slice.8
  415.6 3.9 dynamic_update_slice.8
  436.4 3.9 dynamic_update_slice.8
  442.3 90.9 %all-reduce.6.cloned.1.call-done = (bf16[512,512]{1,0:T(8,128)(2,1)}, bf16[512,512]{1,0:T(8,128)(2,1)}) async-done(((bf16[512,512]{1,0:T(8,128)(2,1)}, bf16[512,512]{1,0:T(8,128)(2,1)}), (bf16[512,512]{1,0:T(8,128)(2,1)}, bf16[512,512]{1,0:T(8,128)(2,1)})) %all-reduce.6.cloned.1.call-update) | async-done | bytes 1048592 | tf_op jit(solution)/shard_map/psum | solution.py:9
  536.5 230.1 %all-reduce.4.cloned.1.call-done = bf16[1024,512]{1,0:T(8,128)(2,1)} async-done(((bf16[1024,512]{1,0:T(8,128)(2,1)}), bf16[1024,512]{1,0:T(8,128)(2,1)}) %all-reduce.4.cloned.1.call-update) | async-done | bytes 1048592 | tf_op jit(solution)/shard_map/psum | solution.py:9
  766.5 3.1 convolution_subtract_fusion
  (172 shorter events, 132.0 us)
Async XLA Ops:
  6.5 88.9 %all-gather.2.cloned.1.call-start = ((), (), s32[]{:S(2)}) async-start(), calls=%async_computation | async-start | bytes 4718592 | tf_op jit(solution)/shard_map/all_gather | solution.py:39
  7.3 8.3 %copy-start.1 = (s32[8,4,2]{0,2,1:T(2,128)S(1)}, s32[8,4,2]{0,2,1:T(2,128)}, u32[]{:S(2)}) copy-start(s32[8,4,2]{0,2,1:T(2,128)} %param.13) | copy-start | bytes 772
  7.3 8.6 %copy-start.2 = (s32[8,4,1]{0,2,1:T(1,128)S(1)}, s32[8,4,1]{0,2,1:T(1,128)}, u32[]{:S(2)}) copy-start(s32[8,4,1]{0,2,1:T(1,128)} %param.12) | copy-start | bytes 388
  15.5 517.7 %all-reduce.6.cloned.1.call-start = ((), (), s32[]{:S(2)}) async-start(), calls=%async_computation.2 | async-start | bytes 2097152 | tf_op jit(solution)/shard_map/psum | solution.py:9
  95.6 344.7 %copy-start = (f32[512,512]{1,0:T(8,128)S(1)}, f32[512,512]{1,0:T(8,128)}, u32[]{:S(2)}) copy-start(f32[512,512]{1,0:T(8,128)} %param.14) | copy-start | bytes 3145732
  442.2 324.3 %all-reduce.4.cloned.1.call-start = ((), (), s32[]{:S(2)}) async-start(), calls=%async_computation.1 | async-start | bytes 2097152 | tf_op jit(solution)/shard_map/psum | solution.py:9
  534.3 232.3 %copy-start.3 = (f32[1024]{0:T(1024)S(1)}, f32[1024]{0:T(1024)}, u32[]{:S(2)}) copy-start(f32[1024]{0:T(1024)} %param.15) | copy-start | bytes 12292
Sparse Core Ops, SparseCore 0:
  15.6 79.8 all-gather.1
  442.4 90.8 all-reduce.5
  536.6 229.9 all-reduce.3
where the time goes:
time: 782 us; the launch traced here: 776 us
  waiting for transfers between devices  400 us (51%)
  local copies, waits for them, and re-layouts  167 us (21%)
  loops' own time  146 us (19%)
  other arithmetic  37.4 us (5%)
  between operations  13.2 us (2%)
  matrix products  11.3 us (1%)
    psum x2, waiting for transfers between devices, spread(): return lax.psum(kept, axis)  321 us
    another operation x1, loops' own time, body(): schur_sum = lax.fori_loop(0, shard_tiles.shape[0], one_tile, zero_sum)  146 us
    dynamic_update_slice x32, local copies, waits for them, and re-layouts, place_tile(): lax.dynamic_update_slice(schur_sum, current + weight * tile_value.astype(...  108 us
    all_gather x1, waiting for transfers between devices, body(): shard_tiles = lax.all_gather(schur_tiles, 'row', axis=0, tiled=True)  79.4 us
    add x32, other arithmetic, place_tile(): current + weight * tile_value.astype(jnp.float32)  33.7 us
    dynamic_slice x32, local copies, waits for them, and re-layouts, one_tile(): row_starts[position]  18.8 us
    dynamic_slice x32, local copies, waits for them, and re-layouts, one_tile(): weight = (targets[position] == my_row).astype(jnp.float32)  18.8 us
    dynamic_slice x32, local copies, waits for them, and re-layouts, one_tile(): col_starts[position]  18.8 us
  transfers between devices with their start and end apart: 3, of which 3 were waited for; matrix products, arithmetic and copies ran while one was open for 0% of the time, Pallas kernels for 0%

commit v1 on v0

v1 whole, which is shorter than its diff:
```python
import jax
import jax.numpy as jnp
from jax import lax
from jax.experimental import pallas as pl
from jax.experimental.pallas import tpu as pltpu
from jax.sharding import PartitionSpec as P

BF = jnp.bfloat16
F32 = jnp.float32
ROWS = ("row", "col")
LIMIT = 48 * 1024 * 1024
OVER_ROWS = (((0,), (0,)), ((), ()))


def tile_kernel(orders, owners, inv_hbm, cpl_hbm, slab, panel_out, tiles_out, inv, cpl, inv_sem, cpl_sem):
    subs = inv_hbm.shape[0]
    me = lax.axis_index("row")
    for s in range(subs):
        pltpu.make_async_copy(cpl_hbm.at[s], cpl.at[s], cpl_sem.at[s]).start()
        pltpu.make_async_copy(inv_hbm.at[s], inv.at[s], inv_sem.at[s]).start()
    for d in range(8):
        for b in range(4):
            panel_out[d, b] = slab[b * 128 + d * 16:b * 128 + d * 16 + 16, :].astype(BF)
        panel_out[d, 4:6] = jnp.zeros((2, 16, 512), BF)
        tiles_out[d, 8:16] = jnp.zeros((8, 16, 512), BF)
    for s in range(subs):
        pltpu.make_async_copy(cpl_hbm.at[s], cpl.at[s], cpl_sem.at[s]).wait()
        pltpu.make_async_copy(inv_hbm.at[s], inv.at[s], inv_sem.at[s]).wait()
        live = lax.broadcasted_iota(jnp.int32, (1024, 256), 0) < orders[0, s]
        masked = jnp.where(live, cpl[s].astype(F32), 0.0).astype(BF)
        solved = jnp.dot(inv[s], masked, preferred_element_type=F32).astype(BF)
        tile = lax.dot_general(masked, solved, OVER_ROWS, preferred_element_type=F32).astype(BF)
        owner = owners[s, me]
        for k in range(8):
            tiles_out[owner, 8 + k, :, 0:256] = tile[k * 16:k * 16 + 16]
            tiles_out[owner, 8 + k, :, 256:512] = tile[128 + k * 16:144 + k * 16]

        @pl.when(owner < 2)
        def _():
            for d in range(8):
                panel_out[d, 4 + owner, :, 0:256] = tile[d * 16:d * 16 + 16]
                panel_out[d, 4 + owner, :, 256:512] = tile[128 + d * 16:144 + d * 16]


def panel_kernel(owners, offsets, piv, got, tiles_in, tiles_out, l0, l1, l2, l3, acc, piece, piv_cols, sems):
    del tiles_in
    me = lax.axis_index("row")
    piv_cols[...] = piv[...].T
    for o in range(2):
        for b in range(4):
            acc[o * 4 + b] = got[o, b].astype(F32)
    for src in range(8):
        for s in range(4):
            owner = owners[s, src]

            @pl.when(owner < 2)
            def _():
                block = owner * 4 + offsets[s, 0, src]
                cols = pl.ds(pl.multiple_of(offsets[s, 1, src] * 128, 128), 256)
                acc[block, :, cols] -= got[src, 4 + owner, :, 0:256].astype(F32)
                acc[block + 1, :, cols] -= got[src, 4 + owner, :, 256:512].astype(F32)
    piece[...] = acc[...].astype(BF)
    copies = [pltpu.make_async_copy(piece, tiles_out.at[d, 0:8], sems.at[d]) for d in range(8)]
    for copy in copies:
        copy.start()
    mine = piv_cols[pl.ds(pl.multiple_of(me * 16, 16), 16), :]
    for block in range(8):
        left = (piece[block].astype(F32) / mine[:, block:block + 1]).astype(BF)
        (l0, l1, l2, l3)[block // 2][block % 2] = left
    for copy in copies:
        copy.wait()


def take_quarter(total, left, panel, z_place, quarter):
    left_rows = left[...].reshape(256, 512)
    right = jnp.concatenate(
        [panel[z_place ^ mask, quarter * 2 + k] for mask in ORDER for k in range(2)], axis=0
    )
    return total - lax.dot_general(left_rows, right, OVER_ROWS, preferred_element_type=F32)


ORDER = (0, 2, 4, 6, 1, 3, 5, 7)


def first_kernel(owners, offsets, slab, got, left_a, left_b, out):
    me = lax.axis_index("row")
    col = lax.axis_index("col")
    z_place, quarter = col // 4, col % 4
    out[...] = slab[...]
    for src in range(8):
        for s in range(4):
            @pl.when(owners[s, src] == me)
            def _():
                row = pl.multiple_of(offsets[s, 0, src] * 128, 128)
                cols = pl.ds(pl.multiple_of(offsets[s, 1, src] * 128, 128), 256)
                block = got[src, 8:16].reshape(128, 512)
                out[pl.ds(row, 128), cols] -= block[:, 0:256].astype(F32)
                out[pl.ds(row + 128, 128), cols] -= block[:, 256:512].astype(F32)
    total = take_quarter(out[...], left_a, got, z_place, quarter)
    out[...] = take_quarter(total, left_b, got, z_place, quarter ^ 1)


def second_kernel(so_far, got, left_a, left_b, out):
    col = lax.axis_index("col")
    z_place, quarter = col // 4, col % 4
    total = take_quarter(so_far[...], left_a, got, z_place, quarter ^ 2)
    out[...] = take_quarter(total, left_b, got, z_place, quarter ^ 3)


def call(kernel, out_shape, in_specs, out_specs, scratch=(), flops=0, nbytes=0, aliases=None):
    return pl.pallas_call(
        kernel,
        out_shape=out_shape,
        in_specs=in_specs,
        out_specs=out_specs,
        scratch_shapes=list(scratch),
        input_output_aliases=aliases or {},
        compiler_params=pltpu.CompilerParams(vmem_limit_bytes=LIMIT),
        cost_estimate=pl.CostEstimate(flops=flops, bytes_accessed=nbytes, transcendentals=0),
    )


VM = pl.BlockSpec(memory_space=pltpu.VMEM)
SM = pl.BlockSpec(memory_space=pltpu.SMEM)
HB = pl.BlockSpec(memory_space=pl.ANY)


def shape(*dims, kind=BF):
    return jax.ShapeDtypeStruct(dims, kind)


def body(inverses, coupling, orders, owners, offsets, dense_slab, pivots):
    owner_rows = owners[:, :, 0].T
    offset_rows = offsets.transpose(1, 2, 0)
    panel_send, tiles_send = call(
        tile_kernel,
        (shape(8, 6, 16, 512), shape(8, 16, 16, 512)),
        [SM, SM, HB, HB, VM],
        (VM, VM),
        (
            pltpu.VMEM((4, 1024, 1024), BF),
            pltpu.VMEM((4, 1024, 256), BF),
            pltpu.SemaphoreType.DMA((4,)),
            pltpu.SemaphoreType.DMA((4,)),
        ),
        2_700_000_000,
        14_000_000,
    )(orders, owner_rows, inverses[0], coupling[0], dense_slab)
    panel_got = lax.all_to_all(panel_send, "row", 0, 0, tiled=True)
    tiles_send, l0, l1, l2, l3 = call(
        panel_kernel,
        (shape(8, 16, 16, 512),) + (shape(2, 16, 512),) * 4,
        [SM, SM, VM, VM, HB],
        (HB, VM, VM, VM, VM),
        (
            pltpu.VMEM((8, 16, 512), F32),
            pltpu.VMEM((8, 16, 512), BF),
            pltpu.VMEM((128, 8), F32),
            pltpu.SemaphoreType.DMA((8,)),
        ),
        1_000_000,
        2_000_000,
        {4: 0},
    )(owner_rows, offset_rows, pivots.reshape(8, 128), panel_got, tiles_send)

    def hop(piece, quarter):
        pairs = [(r * 32 + c, c * 32 + r * 4 + quarter) for r in range(8) for c in range(8)]
        return lax.ppermute(piece, ROWS, pairs)

    def over_col(value, mask):
        return lax.ppermute(value, "col", [(c, c ^ mask) for c in range(32)])

    hops = [hop(piece, quarter) for quarter, piece in enumerate((l0, l1, l2, l3))]
    own = (hops[0] + hops[1]) + (hops[2] + hops[3])
    tiles_send, own = lax.optimization_barrier((tiles_send, own))
    got = lax.all_to_all(tiles_send, "row", 0, 0, tiled=True)
    even = jnp.stack([own] + [over_col(own, 4 * k) for k in (2, 4, 6)])
    left_a = jnp.concatenate([even, over_col(even, 4)])
    left_b = over_col(left_a, 1)
    left_c = over_col(left_a, 2)
    left_d = over_col(left_c, 1)
    partial = call(
        first_kernel, shape(512, 512, kind=F32), [SM, SM, VM, VM, VM, VM], VM, (), 270_000_000, 5_000_000
    )(owner_rows, offset_rows, dense_slab, got, left_a, left_b)
    return call(
        second_kernel, shape(512, 512, kind=F32), [VM, VM, VM, VM], VM, (), 270_000_000, 4_000_000
    )(partial, got, left_c, left_d)


def solution(mesh):
    placed = (
        P("row", "col", None, None),
        P("row", "col", None, None),
        P("row", "col"),
        P(None, "col", None),
        P(None, "col", None),
        P("row", "col"),
        P(),
    )
    return jax.shard_map(
        body, mesh=mesh, in_specs=placed, out_specs=P("row", "col"), check_vma=False
    )
```

time: 782 us -> 102 us (0.13)
  waiting for transfers between devices: 400 us -> 19.5 us
  local copies, waits for them, and re-layouts: 167 us -> 7.17 us
  loops' own time: 146 us -> 0 us
  starting transfers between devices: 0.09 us -> 38.5 us
  other arithmetic: 37.4 us -> 0.03 us
  blocking collectives: 0 us -> 20.8 us
  Pallas kernels: 0 us -> 14.5 us
  between operations: 13.2 us -> 0.16 us
  matrix products: 11.3 us -> 0 us
    psum x2 -> x0, waiting for transfers between devices: 321 us -> none  [spread(): return lax.psum(kept, axis)]
    another operation x1 -> x0, loops' own time: 146 us -> none  [body(): schur_sum = lax.fori_loop(0, shard_tiles.shape[0], one_tile, zero_sum)]
    dynamic_update_slice x32 -> x0, local copies, waits for them, and re-layouts: 108 us -> none  [place_tile(): lax.dynamic_update_slice(schur_sum, current + weight * tile_value.astype(...]
    all_gather x1 -> x0, waiting for transfers between devices: 79.4 us -> none  [body(): shard_tiles = lax.all_gather(schur_tiles, 'row', axis=0, tiled=True)]
    dynamic_slice x96 -> x0, local copies, waits for them, and re-layouts: 56.4 us -> none  [the longest x32 18.8 us: one_tile(): row_starts[position]]
    add x32 -> x1, other arithmetic: 33.7 us -> 0.01 us  [body(): own = hops[0] + hops[1] + (hops[2] + hops[3])]
    ppermute x0 -> x11, starting transfers between devices: none -> 32.1 us  [the longest x4 16.6 us: hop(): return lax.ppermute(piece, ROWS, pairs)]
    all_to_all x0 -> x1, blocking collectives: none -> 20.8 us  [body(): panel_got = lax.all_to_all(panel_send, 'row', 0, 0, tiled=True)]
  transfers between devices with their start and end apart: 3 -> 12, of which waited for: 3 -> 5; matrix products, arithmetic and copies ran while one was open for 0% -> 0% of each run, Pallas kernels for 0% -> 2%
where the time goes in v1:
time: 102 us; the launch traced here: 101 us
  starting transfers between devices  38.5 us (38%)
  blocking collectives  20.8 us (20%)
  waiting for transfers between devices  19.5 us (19%)
  Pallas kernels  14.5 us (14%)
  local copies, waits for them, and re-layouts  7.17 us (7%)
    all_to_all x1, blocking collectives, body(): panel_got = lax.all_to_all(panel_send, 'row', 0, 0, tiled=True)  20.8 us
    ppermute x7, waiting for transfers between devices, over_col(): return lax.ppermute(value, 'col', [(c, c ^ mask) for c in range(32)])  18.5 us
    ppermute x4, starting transfers between devices, hop(): return lax.ppermute(piece, ROWS, pairs)  16.6 us
    ppermute x7, starting transfers between devices, over_col(): return lax.ppermute(value, 'col', [(c, c ^ mask) for c in range(32)])  15.5 us
    pallas_call x1, Pallas kernels, body(): call(tile_kernel, (shape(8, 6, 16, 512), shape(8, 16, 16, 512)), [SM, SM,...  7.95 us
    unnamed x26, local copies, waits for them, and re-layouts  7.16 us
    all_to_all x1, starting transfers between devices, body(): got = lax.all_to_all(tiles_send, 'row', 0, 0, tiled=True)  6.32 us
    pallas_call x1, Pallas kernels, body(): call(panel_kernel, (shape(8, 16, 16, 512),) + (shape(2, 16, 512),) * 4, [...  2.59 us
  transfers between devices with their start and end apart: 12, of which 5 were waited for; matrix products, arithmetic and copies ran while one was open for 0% of the time, Pallas kernels for 2%

profile of v1, /device:TPU:1, one launch (start us, length us, event | category | flops | bytes accessed | tf_op | source)
XLA Modules:
  0.0 100.6 jit_solution(2550530298702664437)
XLA Ops:
  0.0 1.2 %copy-done.1 = f32[512,512]{1,0:T(8,128)S(1)} copy-done((f32[512,512]{1,0:T(8,128)S(1)}, f32[512,512]{1,0:T(8,128)}, u32[]{:S(2)}) %copy-start.1) | copy-done | bytes 1048600
  1.2 1.6 %copy-done.3 = bf16[1,4,1024,256]{3,2,1,0:T(8,128)(2,1)S(1)} copy-done((bf16[1,4,1024,256]{3,2,1,0:T(8,128)(2,1)S(1)}, bf16[1,4,1024,256]{3,2,1,0:T(8,128)(2,1)}, u32[]{:S(2)}) %copy-start.3) | copy-done | bytes 2097176
  4.2 7.9 %shard_map.73 = (bf16[8,6,16,512]{3,2,1,0:T(8,128)(2,1)S(1)}, bf16[8,16,16,512]{3,2,1,0:T(8,128)(2,1)S(1)}) custom-call(s32[1,4]{1,0:T(1,128)S(1)} %copy-done.10, s32[4,8]{1,0:T(4,128)S(1)} %bitcast.16, bf16[4,1024,1024]{2,1,0:T(8,128)(2,1)} %bitcast.22, bf16[4,1024,256]{2,1,0:T(8,128)(2,1)S(1)} %bitcast.15, f32[512,512]{1,0:T(8,128)S(1)} %copy-done.1), custom_call_target="tpu_custom_call" | custom-call | flops 2700000000 | bytes 14000000 | tf_op jit(solution)/shard_map/pallas_call | solution.py:135
  12.1 20.8 %all_to_all.10.got = bf16[8,6,16,512]{3,2,1,0:T(8,128)(2,1)S(1)} all-to-all(bf16[8,6,16,512]{3,2,1,0:T(8,128)(2,1)S(1)} %get-tuple-element.14), channel_id=1, replica_groups=mesh['row'=8,'col'=32] {'row'}, dimensions={0} | all-to-all | bytes 1572864 | tf_op jit(solution)/shard_map/all_to_all | solution.py:149
  32.9 2.6 %shard_map.74 = (bf16[8,16,16,512]{3,2,1,0:T(8,128)(2,1)S(1)}, bf16[2,16,512]{2,1,0:T(8,128)(2,1)S(1)}, bf16[2,16,512]{2,1,0:T(8,128)(2,1)S(1)}, bf16[2,16,512]{2,1,0:T(8,128)(2,1)S(1)}, bf16[2,16,512]{2,1,0:T(8,128)(2,1)S(1)}) custom-call(s32[4,8]{1,0:T(4,128)S(1)} %bitcast.17, s32[4,2,8]{2,1,0:T(2,128)S(1)} %bitcast.19, ...), custom_call_target="tpu_custom_call", output_to_operand_aliasing={{0}: (4, {})} | custom-call | flops 1000000 | bytes 2000000 | tf_op jit(solution)/shard_map/pallas_call | solution.py:150
  35.5 1.3 %copy-done = bf16[8,16,16,512]{3,2,1,0:T(8,128)(2,1)} copy-done((bf16[8,16,16,512]{3,2,1,0:T(8,128)(2,1)}, bf16[8,16,16,512]{3,2,1,0:T(8,128)(2,1)S(1)}, u32[]{:S(2)}) %copy-start) | copy-done | bytes 2097176
  36.8 4.2 %collective-permute-start = (bf16[2,16,512]{2,1,0:T(8,128)(2,1)S(1)}, bf16[2,16,512]{2,1,0:T(8,128)(2,1)S(1)}, u32[]{:S(2)}, u32[]{:S(2)}) collective-permute-start(bf16[2,16,512]{2,1,0:T(8,128)(2,1)S(1)} %get-tuple-element.17), channel_id=1, source_target_pairs={{0,0},{1,32},{2,64},{3,96},{4,128},{5,160},{6,192},{7,224},{32,4},... | collective-permute-start | bytes 98312 | tf_op jit(solution)/shard_map/ppermute | solution.py:168
  41.0 3.5 %collective-permute-start.1 = (bf16[2,16,512]{2,1,0:T(8,128)(2,1)S(1)}, bf16[2,16,512]{2,1,0:T(8,128)(2,1)S(1)}, u32[]{:S(2)}, u32[]{:S(2)}) collective-permute-start(bf16[2,16,512]{2,1,0:T(8,128)(2,1)S(1)} %get-tuple-element.18), channel_id=1, source_target_pairs={{0,1},{1,33},{2,65},{3,97},{4,129},{5,161},{6,193},{7,225},{32,5},... | collective-permute-start | bytes 98312 | tf_op jit(solution)/shard_map/ppermute | solution.py:168
  44.6 5.4 %collective-permute-start.2 = (bf16[2,16,512]{2,1,0:T(8,128)(2,1)S(1)}, bf16[2,16,512]{2,1,0:T(8,128)(2,1)S(1)}, u32[]{:S(2)}, u32[]{:S(2)}) collective-permute-start(bf16[2,16,512]{2,1,0:T(8,128)(2,1)S(1)} %get-tuple-element.19), channel_id=1, source_target_pairs={{0,2},{1,34},{2,66},{3,98},{4,130},{5,162},{6,194},{7,226},{32,6},... | collective-permute-start | bytes 98312 | tf_op jit(solution)/shard_map/ppermute | solution.py:168
  50.0 3.4 %collective-permute-start.3 = (bf16[2,16,512]{2,1,0:T(8,128)(2,1)S(1)}, bf16[2,16,512]{2,1,0:T(8,128)(2,1)S(1)}, u32[]{:S(2)}, u32[]{:S(2)}) collective-permute-start(bf16[2,16,512]{2,1,0:T(8,128)(2,1)S(1)} %get-tuple-element.20), channel_id=1, source_target_pairs={{0,3},{1,35},{2,67},{3,99},{4,131},{5,163},{6,195},{7,227},{32,7},... | collective-permute-start | bytes 98312 | tf_op jit(solution)/shard_map/ppermute | solution.py:168
  53.5 1.0 collective-permute-done.3
  54.5 6.3 %all-to-all-start.1 = ((bf16[8,16,16,512]{3,2,1,0:T(8,128)(2,1)}), bf16[8,16,16,512]{3,2,1,0:T(8,128)(2,1)S(1)}, u32[]{:S(2)}, u32[]{:S(2)}) async-start(bf16[8,16,16,512]{3,2,1,0:T(8,128)(2,1)} %copy-done), calls=%async_computation.1 | async-start | bytes 4194304 | tf_op jit(solution)/shard_map/all_to_all | solution.py:176
  60.8 2.2 %collective-permute-start.5 = (bf16[2,16,512]{2,1,0:T(8,128)(2,1)S(1)}, bf16[2,16,512]{2,1,0:T(8,128)(2,1)S(1)}, u32[]{:S(2)}, u32[]{:S(2)}) collective-permute-start(bf16[2,16,512]{2,1,0:T(8,128)(2,1)S(1)} %add_add_fusion), channel_id=1, source_target_pairs={{0,16},{1,17},{2,18},{3,19},{4,20},{5,21},{6,22},{7,23},{8,24},{9,... | collective-permute-start | bytes 98312 | tf_op jit(solution)/shard_map/ppermute | solution.py:171
  63.0 3.5 %collective-permute-start.4 = (bf16[2,16,512]{2,1,0:T(8,128)(2,1)S(1)}, bf16[2,16,512]{2,1,0:T(8,128)(2,1)S(1)}, u32[]{:S(2)}, u32[]{:S(2)}) collective-permute-start(bf16[2,16,512]{2,1,0:T(8,128)(2,1)S(1)} %add_add_fusion), channel_id=1, source_target_pairs={{0,8},{1,9},{2,10},{3,11},{4,12},{5,13},{6,14},{7,15},{8,0},{9,1},... | collective-permute-start | bytes 98312 | tf_op jit(solution)/shard_map/ppermute | solution.py:171
  66.5 1.1 %collective-permute-done.5 = bf16[2,16,512]{2,1,0:T(8,128)(2,1)S(1)} collective-permute-done((bf16[2,16,512]{2,1,0:T(8,128)(2,1)S(1)}, bf16[2,16,512]{2,1,0:T(8,128)(2,1)S(1)}, u32[]{:S(2)}, u32[]{:S(2)}) %collective-permute-start.5) | collective-permute-done | bytes 32800 | tf_op jit(solution)/shard_map/ppermute | solution.py:171
  67.6 0.8 collective-permute-done.4
  68.5 1.5 %collective-permute-start.7 = (bf16[4,2,16,512]{3,2,1,0:T(8,128)(2,1)S(1)}, bf16[4,2,16,512]{3,2,1,0:T(8,128)(2,1)S(1)}, u32[]{:S(2)}, u32[]{:S(2)}) collective-permute-start(bf16[4,2,16,512]{3,2,1,0:T(8,128)(2,1)S(1)} %pad_maximum_fusion), channel_id=1, source_target_pairs={{0,4},{1,5},{2,6},{3,7},{4,0},{5,1},{6,2},{7,3},{8,12},{9,13},{10,... | collective-permute-start | bytes 393224 | tf_op jit(solution)/shard_map/ppermute | solution.py:171
  70.0 2.6 %collective-permute-done.7 = bf16[4,2,16,512]{3,2,1,0:T(8,128)(2,1)S(1)} collective-permute-done((bf16[4,2,16,512]{3,2,1,0:T(8,128)(2,1)S(1)}, bf16[4,2,16,512]{3,2,1,0:T(8,128)(2,1)S(1)}, u32[]{:S(2)}, u32[]{:S(2)}) %collective-permute-start.7) | collective-permute-done | bytes 131104 | tf_op jit(solution)/shard_map/ppermute | solution.py:171
  72.7 6.4 %collective-permute-start.9 = (bf16[8,2,16,512]{3,2,1,0:T(8,128)(2,1)S(1)}, bf16[8,2,16,512]{3,2,1,0:T(8,128)(2,1)}, u32[]{:S(2)}, u32[]{:S(2)}) collective-permute-start(bf16[8,2,16,512]{3,2,1,0:T(8,128)(2,1)S(1)} %constant_dynamic-update-slice_fusion.left_a), channel_id=1, source_target_pairs={{0,2},{1,3},{2,0},{3,1},{4,6},{5,7},{6,4},{7,5},{8,10},{9,11},{10,... | collective-permute-start | bytes 786440 | tf_op jit(solution)/shard_map/ppermute | solution.py:171
  79.1 1.5 %collective-permute-start.8 = (bf16[8,2,16,512]{3,2,1,0:T(8,128)(2,1)S(1)}, bf16[8,2,16,512]{3,2,1,0:T(8,128)(2,1)S(1)}, u32[]{:S(2)}, u32[]{:S(2)}) collective-permute-start(bf16[8,2,16,512]{3,2,1,0:T(8,128)(2,1)S(1)} %constant_dynamic-update-slice_fusion.left_a), channel_id=1, source_target_pairs={{0,1},{1,0},{2,3},{3,2},{4,5},{5,4},{6,7},{7,6},{8,9},{9,8},{10,11... | collective-permute-start | bytes 786440 | tf_op jit(solution)/shard_map/ppermute | solution.py:171
  80.6 13.9 %collective-permute-done.9.left_a = bf16[8,2,16,512]{3,2,1,0:T(8,128)(2,1)} collective-permute-done((bf16[8,2,16,512]{3,2,1,0:T(8,128)(2,1)S(1)}, bf16[8,2,16,512]{3,2,1,0:T(8,128)(2,1)}, u32[]{:S(2)}, u32[]{:S(2)}) %collective-permute-start.9) | collective-permute-done | bytes 262176 | tf_op jit(solution)/shard_map/ppermute | solution.py:171
  95.7 0.9 copy-done.5
  96.6 1.5 %shard_map.75.so_far = f32[512,512]{1,0:T(8,128)S(1)} custom-call(s32[4,8]{1,0:T(4,128)S(1)} %bitcast.18, s32[4,2,8]{2,1,0:T(2,128)S(1)} %bitcast.20, f32[512,512]{1,0:T(8,128)S(1)} %copy-done.2, bf16[8,16,16,512]{3,2,1,0:T(8,128)(2,1)S(1)} %all-to-all-done.1.got, bf16[8,2,16,512]{3,2,1,0:T(8,128)(2,1)S(1)} %constant_dynamic-update-slice_fusion.left_a, ...), custom_call_target="tpu_custom_call" | custom-call | flops 270000000 | bytes 5000000 | tf_op jit(solution)/shard_map/pallas_call | solution.py:182
  98.2 2.5 %shard_map.76 = f32[512,512]{1,0:T(8,128)} custom-call(f32[512,512]{1,0:T(8,128)S(1)} %shard_map.75.so_far, bf16[8,16,16,512]{3,2,1,0:T(8,128)(2,1)S(1)} %all-to-all-done.1.got, bf16[8,2,16,512]{3,2,1,0:T(8,128)(2,1)} %collective-permute-done.9.left_a, bf16[8,2,16,512]{3,2,1,0:T(8,128)(2,1)} %collective-permute-done.10.left_b), custom_call_target="tpu_custom_call" | custom-call | flops 270000000 | bytes 4000000 | tf_op jit(solution)/shard_map/pallas_call | solution.py:185
  (34 shorter events, 2.5 us)
Async XLA Ops:
  0.0 1.2 %copy-start.1 = (f32[512,512]{1,0:T(8,128)S(1)}, f32[512,512]{1,0:T(8,128)}, u32[]{:S(2)}) copy-start(f32[512,512]{1,0:T(8,128)} %slab.3) | copy-start | bytes 3145732
  1.2 1.6 %copy-start.3 = (bf16[1,4,1024,256]{3,2,1,0:T(8,128)(2,1)S(1)}, bf16[1,4,1024,256]{3,2,1,0:T(8,128)(2,1)}, u32[]{:S(2)}) copy-start(bf16[1,4,1024,256]{3,2,1,0:T(8,128)(2,1)} %param.8) | copy-start | bytes 6291460
  2.8 0.7 copy-start.6
  3.5 0.7 copy-start.10
  4.2 28.7 %copy-start.8 = (s32[8,4,2]{0,2,1:T(2,128)S(1)}, s32[8,4,2]{0,2,1:T(2,128)}, u32[]{:S(2)}) copy-start(s32[8,4,2]{0,2,1:T(2,128)} %param.11) | copy-start | bytes 772
  4.2 28.7 %copy-start.9 = (f32[1024]{0:T(1024)S(1)}, f32[1024]{0:T(1024)}, u32[]{:S(2)}) copy-start(f32[1024]{0:T(1024)} %param.13) | copy-start | bytes 12292
  35.5 1.3 %copy-start = (bf16[8,16,16,512]{3,2,1,0:T(8,128)(2,1)}, bf16[8,16,16,512]{3,2,1,0:T(8,128)(2,1)S(1)}, u32[]{:S(2)}) copy-start(bf16[8,16,16,512]{3,2,1,0:T(8,128)(2,1)S(1)} %get-tuple-element.21) | copy-start | bytes 6291460
  36.8 16.7 %collective-permute-start = (bf16[2,16,512]{2,1,0:T(8,128)(2,1)S(1)}, bf16[2,16,512]{2,1,0:T(8,128)(2,1)S(1)}, u32[]{:S(2)}, u32[]{:S(2)}) collective-permute-start(bf16[2,16,512]{2,1,0:T(8,128)(2,1)S(1)} %get-tuple-element.17), channel_id=1, source_target_pairs={{0,0},{1,32},{2,64},{3,96},{4,128},{5,160},{6,192},{7,224},{32,4},... | collective-permute-start | bytes 98312 | tf_op jit(solution)/shard_map/ppermute | solution.py:168
  41.0 12.4 %collective-permute-start.1 = (bf16[2,16,512]{2,1,0:T(8,128)(2,1)S(1)}, bf16[2,16,512]{2,1,0:T(8,128)(2,1)S(1)}, u32[]{:S(2)}, u32[]{:S(2)}) collective-permute-start(bf16[2,16,512]{2,1,0:T(8,128)(2,1)S(1)} %get-tuple-element.18), channel_id=1, source_target_pairs={{0,1},{1,33},{2,65},{3,97},{4,129},{5,161},{6,193},{7,225},{32,5},... | collective-permute-start | bytes 98312 | tf_op jit(solution)/shard_map/ppermute | solution.py:168
  44.6 8.9 %collective-permute-start.2 = (bf16[2,16,512]{2,1,0:T(8,128)(2,1)S(1)}, bf16[2,16,512]{2,1,0:T(8,128)(2,1)S(1)}, u32[]{:S(2)}, u32[]{:S(2)}) collective-permute-start(bf16[2,16,512]{2,1,0:T(8,128)(2,1)S(1)} %get-tuple-element.19), channel_id=1, source_target_pairs={{0,2},{1,34},{2,66},{3,98},{4,130},{5,162},{6,194},{7,226},{32,6},... | collective-permute-start | bytes 98312 | tf_op jit(solution)/shard_map/ppermute | solution.py:168
  50.0 4.5 %collective-permute-start.3 = (bf16[2,16,512]{2,1,0:T(8,128)(2,1)S(1)}, bf16[2,16,512]{2,1,0:T(8,128)(2,1)S(1)}, u32[]{:S(2)}, u32[]{:S(2)}) collective-permute-start(bf16[2,16,512]{2,1,0:T(8,128)(2,1)S(1)} %get-tuple-element.20), channel_id=1, source_target_pairs={{0,3},{1,35},{2,67},{3,99},{4,131},{5,163},{6,195},{7,227},{32,7},... | collective-permute-start | bytes 98312 | tf_op jit(solution)/shard_map/ppermute | solution.py:168
  54.5 41.2 %copy-start.2 = (f32[512,512]{1,0:T(8,128)S(1)}, f32[512,512]{1,0:T(8,128)}, u32[]{:S(2)}) copy-start(f32[512,512]{1,0:T(8,128)} %slab.3) | copy-start | bytes 3145732
  54.5 41.1 %copy-start.7 = (s32[8,4,1]{0,2,1:T(1,128)S(1)}, s32[8,4,1]{0,2,1:T(1,128)}, u32[]{:S(2)}) copy-start(s32[8,4,1]{0,2,1:T(1,128)} %param.10) | copy-start | bytes 388
  54.5 41.1 %all-to-all-start.1 = ((bf16[8,16,16,512]{3,2,1,0:T(8,128)(2,1)}), bf16[8,16,16,512]{3,2,1,0:T(8,128)(2,1)S(1)}, u32[]{:S(2)}, u32[]{:S(2)}) async-start(bf16[8,16,16,512]{3,2,1,0:T(8,128)(2,1)} %copy-done), calls=%async_computation.1 | async-start | bytes 4194304 | tf_op jit(solution)/shard_map/all_to_all | solution.py:176
  60.8 5.7 %collective-permute-start.6 = (bf16[2,16,512]{2,1,0:T(8,128)(2,1)S(1)}, bf16[2,16,512]{2,1,0:T(8,128)(2,1)S(1)}, u32[]{:S(2)}, u32[]{:S(2)}) collective-permute-start(bf16[2,16,512]{2,1,0:T(8,128)(2,1)S(1)} %add_add_fusion), channel_id=1, source_target_pairs={{0,24},{1,25},{2,26},{3,27},{4,28},{5,29},{6,30},{7,31},{8,16},{9,... | collective-permute-start | bytes 98312 | tf_op jit(solution)/shard_map/ppermute | solution.py:171
  60.8 6.8 %collective-permute-start.5 = (bf16[2,16,512]{2,1,0:T(8,128)(2,1)S(1)}, bf16[2,16,512]{2,1,0:T(8,128)(2,1)S(1)}, u32[]{:S(2)}, u32[]{:S(2)}) collective-permute-start(bf16[2,16,512]{2,1,0:T(8,128)(2,1)S(1)} %add_add_fusion), channel_id=1, source_target_pairs={{0,16},{1,17},{2,18},{3,19},{4,20},{5,21},{6,22},{7,23},{8,24},{9,... | collective-permute-start | bytes 98312 | tf_op jit(solution)/shard_map/ppermute | solution.py:171
  63.0 5.4 %collective-permute-start.4 = (bf16[2,16,512]{2,1,0:T(8,128)(2,1)S(1)}, bf16[2,16,512]{2,1,0:T(8,128)(2,1)S(1)}, u32[]{:S(2)}, u32[]{:S(2)}) collective-permute-start(bf16[2,16,512]{2,1,0:T(8,128)(2,1)S(1)} %add_add_fusion), channel_id=1, source_target_pairs={{0,8},{1,9},{2,10},{3,11},{4,12},{5,13},{6,14},{7,15},{8,0},{9,1},... | collective-permute-start | bytes 98312 | tf_op jit(solution)/shard_map/ppermute | solution.py:171
  68.5 4.2 %collective-permute-start.7 = (bf16[4,2,16,512]{3,2,1,0:T(8,128)(2,1)S(1)}, bf16[4,2,16,512]{3,2,1,0:T(8,128)(2,1)S(1)}, u32[]{:S(2)}, u32[]{:S(2)}) collective-permute-start(bf16[4,2,16,512]{3,2,1,0:T(8,128)(2,1)S(1)} %pad_maximum_fusion), channel_id=1, source_target_pairs={{0,4},{1,5},{2,6},{3,7},{4,0},{5,1},{6,2},{7,3},{8,12},{9,13},{10,... | collective-permute-start | bytes 393224 | tf_op jit(solution)/shard_map/ppermute | solution.py:171
  72.7 21.9 %collective-permute-start.9 = (bf16[8,2,16,512]{3,2,1,0:T(8,128)(2,1)S(1)}, bf16[8,2,16,512]{3,2,1,0:T(8,128)(2,1)}, u32[]{:S(2)}, u32[]{:S(2)}) collective-permute-start(bf16[8,2,16,512]{3,2,1,0:T(8,128)(2,1)S(1)} %constant_dynamic-update-slice_fusion.left_a), channel_id=1, source_target_pairs={{0,2},{1,3},{2,0},{3,1},{4,6},{5,7},{6,4},{7,5},{8,10},{9,11},{10,... | collective-permute-start | bytes 786440 | tf_op jit(solution)/shard_map/ppermute | solution.py:171
  79.1 15.8 %collective-permute-start.8 = (bf16[8,2,16,512]{3,2,1,0:T(8,128)(2,1)S(1)}, bf16[8,2,16,512]{3,2,1,0:T(8,128)(2,1)S(1)}, u32[]{:S(2)}, u32[]{:S(2)}) collective-permute-start(bf16[8,2,16,512]{3,2,1,0:T(8,128)(2,1)S(1)} %constant_dynamic-update-slice_fusion.left_a), channel_id=1, source_target_pairs={{0,1},{1,0},{2,3},{3,2},{4,5},{5,4},{6,7},{7,6},{8,9},{9,8},{10,11... | collective-permute-start | bytes 786440 | tf_op jit(solution)/shard_map/ppermute | solution.py:171
  94.6 3.6 %collective-permute-start.10 = (bf16[8,2,16,512]{3,2,1,0:T(8,128)(2,1)}, bf16[8,2,16,512]{3,2,1,0:T(8,128)(2,1)}, u32[]{:S(2)}, u32[]{:S(2)}) collective-permute-start(bf16[8,2,16,512]{3,2,1,0:T(8,128)(2,1)} %collective-permute-done.9.left_a), channel_id=1, source_target_pairs={{0,1},{1,0},{2,3},{3,2},{4,5},{5,4},{6,7},{7,6},{8,9},{9,8},{10,11... | collective-permute-start | bytes 786440 | tf_op jit(solution)/shard_map/ppermute | solution.py:171
  94.9 0.7 copy-start.4
  95.6 1.0 copy-start.5

commit v2 on v1

v2 whole, which is shorter than its diff:
```python
import jax
import jax.numpy as jnp
from jax import lax
from jax.experimental import pallas as pl
from jax.experimental.pallas import tpu as pltpu
from jax.sharding import PartitionSpec as P

BF = jnp.bfloat16
F32 = jnp.float32
ROWS = ("row", "col")
LIMIT = 32 * 1024 * 1024
WHOLE = 60 * 1024 * 1024
OVER_ROWS = (((0,), (0,)), ((), ()))


def tile_kernel(orders, owners, inv_hbm, cpl_hbm, slab_hbm, send_hbm, keep, inv, cpl, slab, tiles, sems, out_sems):
    me = lax.axis_index("row")
    slab_copy = pltpu.make_async_copy(slab_hbm, slab, sems.at[8])
    cpl_copies = [pltpu.make_async_copy(cpl_hbm.at[s], cpl.at[s], sems.at[s]) for s in range(4)]
    inv_copies = [pltpu.make_async_copy(inv_hbm.at[s], inv.at[s], sems.at[4 + s]) for s in range(4)]
    cpl_copies[0].start()
    inv_copies[0].start()
    slab_copy.start()
    for s in range(1, 4):
        cpl_copies[s].start()
        inv_copies[s].start()
    slab_copy.wait()
    for y in range(4):
        for b in range(4):
            keep[y, b] = slab[b * 128 + y * 32:b * 128 + y * 32 + 32, :].astype(BF)
    copies = []
    for s in range(4):
        cpl_copies[s].wait()
        live = lax.broadcasted_iota(jnp.int32, (1024, 256), 0) < orders[0, s]
        masked = jnp.where(live, cpl[s], jnp.zeros((1024, 256), BF))
        inv_copies[s].wait()
        solved = lax.dot_general(masked, inv[s], OVER_ROWS, preferred_element_type=F32).astype(BF)
        tile = jnp.dot(solved, masked, preferred_element_type=F32).astype(BF)
        owner = owners[s, me]
        for k in range(8):
            tiles[s, k // 2, k % 2, :, 0:256] = tile[k * 16:k * 16 + 16]
            tiles[s, k // 2, k % 2, :, 256:512] = tile[128 + k * 16:144 + k * 16]
        copy = pltpu.make_async_copy(tiles.at[s], send_hbm.at[owner // 2, owner % 2, 1:5], out_sems.at[s])
        copy.start()
        copies.append(copy)
        panel_copy = pltpu.make_async_copy(tiles.at[s], send_hbm.at[:, owner % 2, 0], out_sems.at[4 + s])
        copies.append((owner, panel_copy))

        @pl.when(owner < 2)
        def _():
            panel_copy.start()

    for copy in copies:
        if isinstance(copy, tuple):
            pl.when(copy[0] < 2)(copy[1].wait)
        else:
            copy.wait()


def panel_kernel(owners, offsets, piv, got, keep, far_a, far_b, far_c, piece, left, acc, piv_cols):
    me = lax.axis_index("row")
    place = me // 2
    piv_cols[...] = piv[...].T

    @pl.when(place == 0)
    def _():
        acc[...] = keep[0].astype(F32)

    for y, far in enumerate((far_a, far_b, far_c)):
        @pl.when(place == y + 1)
        def _():
            acc[...] = far[...].astype(F32)

    for src in range(8):
        for s in range(4):
            @pl.when(owners[s, src] == me % 2)
            def _():
                block = offsets[s, 0, src]
                cols = pl.ds(pl.multiple_of(offsets[s, 1, src] * 128, 128), 256)
                rows = got[src, 0].reshape(32, 512).astype(F32)
                acc[block, :, cols] -= rows[:, 0:256]
                acc[block + 1, :, cols] -= rows[:, 256:512]
    piece[...] = acc[...].astype(BF)
    mine = piv_cols[pl.ds(pl.multiple_of(place * 32, 32), 32), :]
    first = me % 2 == 0
    for b in range(4):
        column = jnp.where(first, mine[:, b:b + 1], mine[:, 4 + b:5 + b])
        left[b] = (piece[b].astype(F32) / column).astype(BF)


def take(total, left, panel, mask):
    me = lax.axis_index("row")
    col = lax.axis_index("col")
    row = ((col // 4) & 4) | ((col & 3) ^ mask)
    right = jnp.concatenate([panel[row ^ me].reshape(128, 512), panel[row ^ me ^ 4].reshape(128, 512)], axis=0)
    return total - lax.dot_general(
        left[...].reshape(256, 512), right, OVER_ROWS, preferred_element_type=F32
    )


def base_kernel(owners, offsets, slab, tiles, out):
    me = lax.axis_index("row")
    out[...] = slab[...]
    for src in range(8):
        for s in range(4):
            @pl.when(owners[s, src] == me)
            def _():
                row = pl.multiple_of(offsets[s, 0, src] * 128, 128)
                cols = pl.ds(pl.multiple_of(offsets[s, 1, src] * 128, 128), 256)
                block = tiles[src, 1:5].reshape(128, 512)
                out[pl.ds(row, 128), cols] -= block[:, 0:256].astype(F32)
                out[pl.ds(row + 128, 128), cols] -= block[:, 256:512].astype(F32)


def middle_kernel(base, got, left_a, left_b, left_c, out):
    total = take(base[...], left_a, got, 0)
    out[...] = take(take(total, left_b, got, 1), left_c, got, 2)


def last_kernel(so_far, got, left, out):
    out[...] = take(so_far[...], left, got, 3)


def call(kernel, out_shape, in_specs, out_specs, scratch=(), flops=0, nbytes=0, aliases=None, limit=LIMIT):
    return pl.pallas_call(
        kernel,
        out_shape=out_shape,
        in_specs=in_specs,
        out_specs=out_specs,
        scratch_shapes=list(scratch),
        input_output_aliases=aliases or {},
        compiler_params=pltpu.CompilerParams(vmem_limit_bytes=limit),
        cost_estimate=pl.CostEstimate(flops=flops, bytes_accessed=nbytes, transcendentals=0),
    )


VM = pl.BlockSpec(memory_space=pltpu.VMEM)
SM = pl.BlockSpec(memory_space=pltpu.SMEM)
HB = pl.BlockSpec(memory_space=pltpu.HBM)


def shape(*dims, kind=BF):
    return jax.ShapeDtypeStruct(dims, kind)


def body(inverses, coupling, orders, owners, offsets, dense_slab, pivots):
    owner_rows = owners[:, :, 0].T
    offset_rows = offsets.transpose(1, 2, 0)
    send, keep = call(
        tile_kernel,
        (shape(4, 2, 5, 2, 16, 512), shape(4, 4, 32, 512)),
        [SM, SM, HB, HB, HB],
        (HB, VM),
        (
            pltpu.VMEM((4, 1024, 1024), BF),
            pltpu.VMEM((4, 1024, 256), BF),
            pltpu.VMEM((512, 512), F32),
            pltpu.VMEM((4, 4, 2, 16, 512), BF),
            pltpu.SemaphoreType.DMA((9,)),
            pltpu.SemaphoreType.DMA((8,)),
        ),
        2_700_000_000,
        14_000_000,
        limit=WHOLE,
    )(orders, owner_rows, inverses[0], coupling[0], dense_slab)
    tiles = lax.all_to_all(send.reshape(8, 5, 2, 16, 512), "row", 0, 0, tiled=True)
    far = [lax.ppermute(keep[k], "row", [(0, 2 * k), (1, 2 * k + 1)]) for k in range(1, 4)]
    piece, left = call(
        panel_kernel,
        (shape(4, 32, 512), shape(4, 32, 512)),
        [SM, SM] + [VM] * 6,
        (VM, VM),
        (pltpu.VMEM((4, 32, 512), F32), pltpu.VMEM((128, 8), F32)),
        1_000_000,
        2_000_000,
    )(owner_rows, offset_rows, pivots.reshape(8, 128), tiles, keep, *far)

    def hop(mask):
        pairs = [(r * 32 + c, c * 32 + (r ^ mask) * 4 + (r & 3)) for r in range(8) for c in range(8)]
        return lax.ppermute(left, ROWS, pairs)

    def spread(value, mask):
        return lax.ppermute(value, "col", [(z * 4 + (z & 3), (z ^ mask) * 4 + (z & 3)) for z in range(8)])

    def over_col(value, mask):
        return lax.ppermute(value, "col", [(c, c ^ mask) for c in range(32)])

    def over_row(value, mask):
        return lax.ppermute(value, "row", [(r, r ^ mask) for r in range(8)])

    pair = jnp.stack([hop(0), hop(4)])
    across = jnp.stack([piece, over_row(piece, 1)])
    got = jnp.concatenate([across] + [over_row(across, 2 * k) for k in range(1, 4)])
    left_a = (pair + spread(pair, 1)) + (spread(pair, 2) + spread(pair, 3))
    left_b = over_col(left_a, 1)
    left_c = over_col(left_a, 2)
    left_d = over_col(left_c, 1)
    full = shape(512, 512, kind=F32)
    base = call(base_kernel, full, [SM, SM, VM, VM], VM, (), 1_000_000, 3_000_000)(
        owner_rows, offset_rows, dense_slab, tiles
    )
    total = call(middle_kernel, full, [VM] * 5, VM, (), 400_000_000, 4_000_000)(base, got, left_a, left_b, left_c)
    return call(last_kernel, full, [VM] * 3, VM, (), 135_000_000, 3_000_000)(total, got, left_d)


def solution(mesh):
    placed = (
        P("row", "col", None, None),
        P("row", "col", None, None),
        P("row", "col"),
        P(None, "col", None),
        P(None, "col", None),
        P("row", "col"),
        P(),
    )
    return jax.shard_map(
        body, mesh=mesh, in_specs=placed, out_specs=P("row", "col"), check_vma=False
    )
```

time: 102 us -> 83 us (0.81)
  blocking collectives: 20.8 us -> 0 us
  waiting for transfers between devices: 19.5 us -> 29.2 us
  local copies, waits for them, and re-layouts: 7.17 us -> 0.13 us
  Pallas kernels: 14.5 us -> 13 us
  starting transfers between devices: 38.5 us -> 39.9 us
    ppermute x4 -> x12, waiting for transfers between devices: 0.98 us -> 21.8 us  [the longest x3 12.1 us: body(): lax.ppermute(keep[k], 'row', [(0, 2 * k), (1, 2 * k + 1)])]
    all_to_all x1 -> x0, blocking collectives: 20.8 us -> none  [body(): panel_got = lax.all_to_all(panel_send, 'row', 0, 0, tiled=True)]
    ppermute x4 -> x12, starting transfers between devices: 16.6 us -> 31.1 us  [the longest x2 14.5 us: hop(): return lax.ppermute(left, ROWS, pairs)]
    ppermute x7 -> x3, starting transfers between devices: 15.5 us -> 1.28 us  [over_col(): return lax.ppermute(value, 'col', [(c, c ^ mask) for c in range(32)])]
    ppermute x7 -> x3, waiting for transfers between devices: 18.5 us -> 7.39 us  [over_col(): return lax.ppermute(value, 'col', [(c, c ^ mask) for c in range(32)])]
    unnamed x26 -> x14, local copies, waits for them, and re-layouts: 7.16 us -> 0.09 us
    pallas_call x4 -> x5, Pallas kernels: 14.5 us -> 13 us  [the longest x1 8.8 us: body(): call(tile_kernel, (shape(4, 2, 5, 2, 16, 512), shape(4, 4, 32, 512)), [SM...]
    all_to_all x1, starting transfers between devices: 6.32 us -> 7.54 us  [body(): lax.all_to_all(send.reshape(8, 5, 2, 16, 512), 'row', 0, 0, tiled=True)]
  transfers between devices with their start and end apart: 12 -> 16, of which waited for: 5 -> 5; matrix products, arithmetic and copies ran while one was open for 0% -> 0% of each run, Pallas kernels for 2% -> 2%
where the time goes in v2:
time: 83 us; the launch traced here: 82.6 us
  starting transfers between devices  39.9 us (48%)
  waiting for transfers between devices  29.2 us (35%)
  Pallas kernels  13 us (16%)
    ppermute x2, starting transfers between devices, hop(): return lax.ppermute(left, ROWS, pairs)  14.5 us
    ppermute x3, waiting for transfers between devices, body(): lax.ppermute(keep[k], 'row', [(0, 2 * k), (1, 2 * k + 1)])  12.1 us
    ppermute x3, waiting for transfers between devices, spread(): lax.ppermute(value, 'col', [(z * 4 + (z & 3), (z ^ mask) * 4 + (z & 3)) f...  9.61 us
    pallas_call x1, Pallas kernels, body(): call(tile_kernel, (shape(4, 2, 5, 2, 16, 512), shape(4, 4, 32, 512)), [SM...  8.8 us
    all_to_all x1, starting transfers between devices, body(): lax.all_to_all(send.reshape(8, 5, 2, 16, 512), 'row', 0, 0, tiled=True)  7.54 us
    ppermute x3, waiting for transfers between devices, over_col(): return lax.ppermute(value, 'col', [(c, c ^ mask) for c in range(32)])  7.39 us
    ppermute x4, starting transfers between devices, over_row(): return lax.ppermute(value, 'row', [(r, r ^ mask) for r in range(8)])  7 us
    ppermute x3, starting transfers between devices, body(): lax.ppermute(keep[k], 'row', [(0, 2 * k), (1, 2 * k + 1)])  6.96 us
  transfers between devices with their start and end apart: 16, of which 5 were waited for; matrix products, arithmetic and copies ran while one was open for 0% of the time, Pallas kernels for 2%

profile of v2, /device:TPU:1, one launch (start us, length us, event | category | flops | bytes accessed | tf_op | source)
XLA Modules:
  0.0 82.6 jit_solution(12144035160593818857)
XLA Ops:
  0.0 8.8 %shard_map.73 = (bf16[4,2,5,2,16,512]{5,4,3,2,1,0:T(8,128)(2,1)}, bf16[4,4,32,512]{3,2,1,0:T(8,128)(2,1)}) custom-call(s32[1,4]{1,0:T(1,128)} %orders.1, s32[4,8]{1,0:T(4,128)} %bitcast.21, bf16[4,1024,1024]{2,1,0:T(8,128)(2,1)} %bitcast.27, bf16[4,1024,256]{2,1,0:T(8,128)(2,1)} %bitcast.28, f32[512,512]{1,0:T(8,128)} %slab.1), custom_call_target="tpu_custom_call" | custom-call | flops 2700000000 | bytes 14000000 | tf_op jit(solution)/shard_map/pallas_call | solution.py:149
  8.9 7.5 %all-to-all-start = ((bf16[8,5,2,16,512]{4,3,2,1,0:T(8,128)(2,1)}), bf16[8,5,2,16,512]{4,3,2,1,0:T(8,128)(2,1)S(1)}, u32[]{:S(2)}, u32[]{:S(2)}) async-start(bf16[8,5,2,16,512]{4,3,2,1,0:T(8,128)(2,1)} %bitcast.29), calls=%async_computation | async-start | bytes 2621440 | tf_op jit(solution)/shard_map/all_to_all | solution.py:166
  16.4 3.5 %collective-permute-start = (bf16[4,32,512]{2,1,0:T(8,128)(2,1)S(1)}, bf16[4,32,512]{2,1,0:T(8,128)(2,1)S(1)}, u32[]{:S(2)}, u32[]{:S(2)}) collective-permute-start(bf16[4,32,512]{2,1,0:T(8,128)(2,1)S(1)} %get-tuple-element.15), channel_id=1, source_target_pairs={{0,64},{32,96},{1,65},{33,97},{2,66},{34,98},{3,67},{35,99},{4,68}... | collective-permute-start | bytes 393224 | tf_op jit(solution)/shard_map/ppermute | solution.py:167
  19.9 2.2 %collective-permute-start.1 = (bf16[4,32,512]{2,1,0:T(8,128)(2,1)S(1)}, bf16[4,32,512]{2,1,0:T(8,128)(2,1)S(1)}, u32[]{:S(2)}, u32[]{:S(2)}) collective-permute-start(bf16[4,32,512]{2,1,0:T(8,128)(2,1)S(1)} %get-tuple-element.14), channel_id=1, source_target_pairs={{0,128},{32,160},{1,129},{33,161},{2,130},{34,162},{3,131},{35,163... | collective-permute-start | bytes 393224 | tf_op jit(solution)/shard_map/ppermute | solution.py:167
  22.1 1.3 %collective-permute-start.2 = (bf16[4,32,512]{2,1,0:T(8,128)(2,1)S(1)}, bf16[4,32,512]{2,1,0:T(8,128)(2,1)S(1)}, u32[]{:S(2)}, u32[]{:S(2)}) collective-permute-start(bf16[4,32,512]{2,1,0:T(8,128)(2,1)S(1)} %get-tuple-element.13), channel_id=1, source_target_pairs={{0,192},{32,224},{1,193},{33,225},{2,194},{34,226},{3,195},{35,227... | collective-permute-start | bytes 393224 | tf_op jit(solution)/shard_map/ppermute | solution.py:167
  23.4 5.8 %collective-permute-done.far_a = bf16[4,32,512]{2,1,0:T(8,128)(2,1)S(1)} collective-permute-done((bf16[4,32,512]{2,1,0:T(8,128)(2,1)S(1)}, bf16[4,32,512]{2,1,0:T(8,128)(2,1)S(1)}, u32[]{:S(2)}, u32[]{:S(2)}) %collective-permute-start) | collective-permute-done | bytes 131104 | tf_op jit(solution)/shard_map/ppermute | solution.py:167
  29.2 6.4 %collective-permute-done.1.far_b = bf16[4,32,512]{2,1,0:T(8,128)(2,1)S(1)} collective-permute-done((bf16[4,32,512]{2,1,0:T(8,128)(2,1)S(1)}, bf16[4,32,512]{2,1,0:T(8,128)(2,1)S(1)}, u32[]{:S(2)}, u32[]{:S(2)}) %collective-permute-start.1) | collective-permute-done | bytes 131104 | tf_op jit(solution)/shard_map/ppermute | solution.py:167
  35.6 1.2 %shard_map.75 = (bf16[4,32,512]{2,1,0:T(8,128)(2,1)S(1)}, bf16[4,32,512]{2,1,0:T(8,128)(2,1)S(1)}) custom-call(s32[4,8]{1,0:T(4,128)S(1)} %bitcast.22, s32[4,2,8]{2,1,0:T(2,128)S(1)} %bitcast.24, f32[8,128]{1,0:T(8,128)S(1)} %bitcast.26, bf16[8,5,2,16,512]{4,3,2,1,0:T(8,128)(2,1)S(1)} %all-to-all-done.tiles.got, bf16[4,4,32,512]{3,2,1,0:T(8,128)(2,1)S(1)} %copy-done.1, ...), custom_call_target="tpu_custom_call" | custom-call | flops 1000000 | bytes 2000000 | tf_op jit(solution)/shard_map/pallas_call | solution.py:168
  36.8 13.2 %collective-permute-start.8 = (bf16[4,32,512]{2,1,0:T(8,128)(2,1)S(1)}, bf16[4,32,512]{2,1,0:T(8,128)(2,1)S(1)}, u32[]{:S(2)}, u32[]{:S(2)}) collective-permute-start(bf16[4,32,512]{2,1,0:T(8,128)(2,1)S(1)} %get-tuple-element.12), channel_id=1, source_target_pairs={{0,16},{1,48},{2,80},{3,112},{4,144},{5,176},{6,208},{7,240},{32,2... | collective-permute-start | bytes 393224 | tf_op jit(solution)/shard_map/ppermute | solution.py:180
  50.0 1.3 %collective-permute-start.7 = (bf16[4,32,512]{2,1,0:T(8,128)(2,1)S(1)}, bf16[4,32,512]{2,1,0:T(8,128)(2,1)S(1)}, u32[]{:S(2)}, u32[]{:S(2)}) collective-permute-start(bf16[4,32,512]{2,1,0:T(8,128)(2,1)S(1)} %get-tuple-element.12), channel_id=1, source_target_pairs={{0,0},{1,32},{2,64},{3,96},{4,128},{5,160},{6,192},{7,224},{32,5},... | collective-permute-start | bytes 393224 | tf_op jit(solution)/shard_map/ppermute | solution.py:180
  51.3 3.1 %collective-permute-start.3 = (bf16[4,32,512]{2,1,0:T(8,128)(2,1)S(1)}, bf16[4,32,512]{2,1,0:T(8,128)(2,1)S(1)}, u32[]{:S(2)}, u32[]{:S(2)}) collective-permute-start(bf16[4,32,512]{2,1,0:T(8,128)(2,1)S(1)} %get-tuple-element.11), channel_id=1, source_target_pairs={{0,32},{32,0},{64,96},{96,64},{128,160},{160,128},{192,224},{224,1... | collective-permute-start | bytes 393224 | tf_op jit(solution)/shard_map/ppermute | solution.py:189
  54.4 1.1 %shard_map.74.base = f32[512,512]{1,0:T(8,128)S(1)} custom-call(s32[4,8]{1,0:T(4,128)S(1)} %bitcast.23, s32[4,2,8]{2,1,0:T(2,128)S(1)} %bitcast.25, f32[512,512]{1,0:T(8,128)S(1)} %copy-done, bf16[8,5,2,16,512]{4,3,2,1,0:T(8,128)(2,1)S(1)} %all-to-all-done.tiles.got), custom_call_target="tpu_custom_call" | custom-call | flops 1000000 | bytes 3000000 | tf_op jit(solution)/shard_map/pallas_call | solution.py:199
  55.6 0.7 collective-permute-start.10
  56.2 0.7 collective-permute-start.11
  56.9 1.3 %collective-permute-start.9 = (bf16[2,4,32,512]{3,2,1,0:T(8,128)(2,1)S(1)}, bf16[2,4,32,512]{3,2,1,0:T(8,128)(2,1)S(1)}, u32[]{:S(2)}, u32[]{:S(2)}) collective-permute-start(bf16[2,4,32,512]{3,2,1,0:T(8,128)(2,1)S(1)} %pad_maximum_fusion.1), channel_id=1, source_target_pairs={{0,4},{5,1},{10,14},{15,11},{16,20},{21,17},{26,30},{31,27},{32,36... | collective-permute-start | bytes 786440 | tf_op jit(solution)/shard_map/ppermute | solution.py:183
  58.4 2.9 %collective-permute-start.5 = (bf16[2,4,32,512]{3,2,1,0:T(8,128)(2,1)S(1)}, bf16[2,4,32,512]{3,2,1,0:T(8,128)(2,1)S(1)}, u32[]{:S(2)}, u32[]{:S(2)}) collective-permute-start(bf16[2,4,32,512]{3,2,1,0:T(8,128)(2,1)S(1)} %pad_maximum_fusion), channel_id=1, source_target_pairs={{0,128},{32,160},{64,192},{96,224},{128,0},{160,32},{192,64},{224,... | collective-permute-start | bytes 786440 | tf_op jit(solution)/shard_map/ppermute | solution.py:189
  61.3 1.0 %collective-permute-start.6 = (bf16[2,4,32,512]{3,2,1,0:T(8,128)(2,1)S(1)}, bf16[2,4,32,512]{3,2,1,0:T(8,128)(2,1)S(1)}, u32[]{:S(2)}, u32[]{:S(2)}) collective-permute-start(bf16[2,4,32,512]{3,2,1,0:T(8,128)(2,1)S(1)} %pad_maximum_fusion), channel_id=1, source_target_pairs={{0,192},{32,224},{64,128},{96,160},{128,64},{160,96},{192,0},{224,... | collective-permute-start | bytes 786440 | tf_op jit(solution)/shard_map/ppermute | solution.py:189
  62.2 9.6 %collective-permute-done.9 = bf16[2,4,32,512]{3,2,1,0:T(8,128)(2,1)S(1)} collective-permute-done((bf16[2,4,32,512]{3,2,1,0:T(8,128)(2,1)S(1)}, bf16[2,4,32,512]{3,2,1,0:T(8,128)(2,1)S(1)}, u32[]{:S(2)}, u32[]{:S(2)}) %collective-permute-start.9) | collective-permute-done | bytes 262176 | tf_op jit(solution)/shard_map/ppermute | solution.py:183
  72.0 0.8 collective-permute-start.12
  72.8 6.9 %collective-permute-done.13.left_c = bf16[2,4,32,512]{3,2,1,0:T(8,128)(2,1)S(1)} collective-permute-done((bf16[2,4,32,512]{3,2,1,0:T(8,128)(2,1)S(1)}, bf16[2,4,32,512]{3,2,1,0:T(8,128)(2,1)S(1)}, u32[]{:S(2)}, u32[]{:S(2)}) %collective-permute-start.13) | collective-permute-done | bytes 262176 | tf_op jit(solution)/shard_map/ppermute | solution.py:186
  79.8 0.4 collective-permute-start.14
  80.2 0.6 shard_map.76.so_far
  80.8 0.5 collective-permute-done.14.left
  81.3 1.3 %shard_map.77 = f32[512,512]{1,0:T(8,128)} custom-call(f32[512,512]{1,0:T(8,128)S(1)} %shard_map.76.so_far, bf16[8,4,32,512]{3,2,1,0:T(8,128)(2,1)S(1)} %constant_dynamic-update-slice_fusion.got, bf16[2,4,32,512]{3,2,1,0:T(8,128)(2,1)S(1)} %collective-permute-done.14.left), custom_call_target="tpu_custom_call" | custom-call | flops 135000000 | bytes 3000000 | tf_op jit(solution)/shard_map/pallas_call | solution.py:203
  (32 shorter events, 0.5 us)
Async XLA Ops:
  8.8 7.6 %copy-start.1 = (bf16[4,4,32,512]{3,2,1,0:T(8,128)(2,1)S(1)}, bf16[4,4,32,512]{3,2,1,0:T(8,128)(2,1)}, u32[]{:S(2)}) copy-start(bf16[4,4,32,512]{3,2,1,0:T(8,128)(2,1)} %get-tuple-element.10.keep) | copy-start | bytes 1572868
  8.8 26.8 %copy-start.2 = (s32[8,4,1]{0,2,1:T(1,128)S(1)}, s32[8,4,1]{0,2,1:T(1,128)}, u32[]{:S(2)}) copy-start(s32[8,4,1]{0,2,1:T(1,128)} %param.10) | copy-start | bytes 388
  8.8 26.8 %copy-start.3 = (s32[8,4,2]{0,2,1:T(2,128)S(1)}, s32[8,4,2]{0,2,1:T(2,128)}, u32[]{:S(2)}) copy-start(s32[8,4,2]{0,2,1:T(2,128)} %param.11) | copy-start | bytes 772
  8.8 26.8 %copy-start.4 = (f32[1024]{0:T(1024)S(1)}, f32[1024]{0:T(1024)}, u32[]{:S(2)}) copy-start(f32[1024]{0:T(1024)} %param.13) | copy-start | bytes 12292
  8.9 26.7 %all-to-all-start = ((bf16[8,5,2,16,512]{4,3,2,1,0:T(8,128)(2,1)}), bf16[8,5,2,16,512]{4,3,2,1,0:T(8,128)(2,1)S(1)}, u32[]{:S(2)}, u32[]{:S(2)}) async-start(bf16[8,5,2,16,512]{4,3,2,1,0:T(8,128)(2,1)} %bitcast.29), calls=%async_computation | async-start | bytes 2621440 | tf_op jit(solution)/shard_map/all_to_all | solution.py:166
  16.4 38.0 %copy-start = (f32[512,512]{1,0:T(8,128)S(1)}, f32[512,512]{1,0:T(8,128)}, u32[]{:S(2)}) copy-start(f32[512,512]{1,0:T(8,128)} %slab.1) | copy-start | bytes 3145732
  16.4 12.8 %collective-permute-start = (bf16[4,32,512]{2,1,0:T(8,128)(2,1)S(1)}, bf16[4,32,512]{2,1,0:T(8,128)(2,1)S(1)}, u32[]{:S(2)}, u32[]{:S(2)}) collective-permute-start(bf16[4,32,512]{2,1,0:T(8,128)(2,1)S(1)} %get-tuple-element.15), channel_id=1, source_target_pairs={{0,64},{32,96},{1,65},{33,97},{2,66},{34,98},{3,67},{35,99},{4,68}... | collective-permute-start | bytes 393224 | tf_op jit(solution)/shard_map/ppermute | solution.py:167
  19.9 15.6 %collective-permute-start.1 = (bf16[4,32,512]{2,1,0:T(8,128)(2,1)S(1)}, bf16[4,32,512]{2,1,0:T(8,128)(2,1)S(1)}, u32[]{:S(2)}, u32[]{:S(2)}) collective-permute-start(bf16[4,32,512]{2,1,0:T(8,128)(2,1)S(1)} %get-tuple-element.14), channel_id=1, source_target_pairs={{0,128},{32,160},{1,129},{33,161},{2,130},{34,162},{3,131},{35,163... | collective-permute-start | bytes 393224 | tf_op jit(solution)/shard_map/ppermute | solution.py:167
  22.1 13.4 %collective-permute-start.2 = (bf16[4,32,512]{2,1,0:T(8,128)(2,1)S(1)}, bf16[4,32,512]{2,1,0:T(8,128)(2,1)S(1)}, u32[]{:S(2)}, u32[]{:S(2)}) collective-permute-start(bf16[4,32,512]{2,1,0:T(8,128)(2,1)S(1)} %get-tuple-element.13), channel_id=1, source_target_pairs={{0,192},{32,224},{1,193},{33,225},{2,194},{34,226},{3,195},{35,227... | collective-permute-start | bytes 393224 | tf_op jit(solution)/shard_map/ppermute | solution.py:167
  36.8 18.7 %collective-permute-start.8 = (bf16[4,32,512]{2,1,0:T(8,128)(2,1)S(1)}, bf16[4,32,512]{2,1,0:T(8,128)(2,1)S(1)}, u32[]{:S(2)}, u32[]{:S(2)}) collective-permute-start(bf16[4,32,512]{2,1,0:T(8,128)(2,1)S(1)} %get-tuple-element.12), channel_id=1, source_target_pairs={{0,16},{1,48},{2,80},{3,112},{4,144},{5,176},{6,208},{7,240},{32,2... | collective-permute-start | bytes 393224 | tf_op jit(solution)/shard_map/ppermute | solution.py:180
  50.0 5.5 %collective-permute-start.7 = (bf16[4,32,512]{2,1,0:T(8,128)(2,1)S(1)}, bf16[4,32,512]{2,1,0:T(8,128)(2,1)S(1)}, u32[]{:S(2)}, u32[]{:S(2)}) collective-permute-start(bf16[4,32,512]{2,1,0:T(8,128)(2,1)S(1)} %get-tuple-element.12), channel_id=1, source_target_pairs={{0,0},{1,32},{2,64},{3,96},{4,128},{5,160},{6,192},{7,224},{32,5},... | collective-permute-start | bytes 393224 | tf_op jit(solution)/shard_map/ppermute | solution.py:180
  51.3 6.9 %collective-permute-start.3 = (bf16[4,32,512]{2,1,0:T(8,128)(2,1)S(1)}, bf16[4,32,512]{2,1,0:T(8,128)(2,1)S(1)}, u32[]{:S(2)}, u32[]{:S(2)}) collective-permute-start(bf16[4,32,512]{2,1,0:T(8,128)(2,1)S(1)} %get-tuple-element.11), channel_id=1, source_target_pairs={{0,32},{32,0},{64,96},{96,64},{128,160},{160,128},{192,224},{224,1... | collective-permute-start | bytes 393224 | tf_op jit(solution)/shard_map/ppermute | solution.py:189
  55.6 5.7 %collective-permute-start.10 = (bf16[2,4,32,512]{3,2,1,0:T(8,128)(2,1)S(1)}, bf16[2,4,32,512]{3,2,1,0:T(8,128)(2,1)S(1)}, u32[]{:S(2)}, u32[]{:S(2)}) collective-permute-start(bf16[2,4,32,512]{3,2,1,0:T(8,128)(2,1)S(1)} %pad_maximum_fusion.1), channel_id=1, source_target_pairs={{0,8},{5,13},{10,2},{15,7},{16,24},{21,29},{26,18},{31,23},{32,40}... | collective-permute-start | bytes 786440 | tf_op jit(solution)/shard_map/ppermute | solution.py:183
  56.2 6.0 %collective-permute-start.11 = (bf16[2,4,32,512]{3,2,1,0:T(8,128)(2,1)S(1)}, bf16[2,4,32,512]{3,2,1,0:T(8,128)(2,1)S(1)}, u32[]{:S(2)}, u32[]{:S(2)}) collective-permute-start(bf16[2,4,32,512]{3,2,1,0:T(8,128)(2,1)S(1)} %pad_maximum_fusion.1), channel_id=1, source_target_pairs={{0,12},{5,9},{10,6},{15,3},{16,28},{21,25},{26,22},{31,19},{32,44}... | collective-permute-start | bytes 786440 | tf_op jit(solution)/shard_map/ppermute | solution.py:183
  56.9 14.9 %collective-permute-start.9 = (bf16[2,4,32,512]{3,2,1,0:T(8,128)(2,1)S(1)}, bf16[2,4,32,512]{3,2,1,0:T(8,128)(2,1)S(1)}, u32[]{:S(2)}, u32[]{:S(2)}) collective-permute-start(bf16[2,4,32,512]{3,2,1,0:T(8,128)(2,1)S(1)} %pad_maximum_fusion.1), channel_id=1, source_target_pairs={{0,4},{5,1},{10,14},{15,11},{16,20},{21,17},{26,30},{31,27},{32,36... | collective-permute-start | bytes 786440 | tf_op jit(solution)/shard_map/ppermute | solution.py:183
  58.3 14.5 %collective-permute-start.4 = (bf16[2,4,32,512]{3,2,1,0:T(8,128)(2,1)S(1)}, bf16[2,4,32,512]{3,2,1,0:T(8,128)(2,1)S(1)}, u32[]{:S(2)}, u32[]{:S(2)}) collective-permute-start(bf16[2,4,32,512]{3,2,1,0:T(8,128)(2,1)S(1)} %pad_maximum_fusion), channel_id=1, source_target_pairs={{0,64},{32,96},{64,0},{96,32},{128,192},{160,224},{192,128},{224,1... | collective-permute-start | bytes 786440 | tf_op jit(solution)/shard_map/ppermute | solution.py:189
  58.4 21.8 %collective-permute-start.5 = (bf16[2,4,32,512]{3,2,1,0:T(8,128)(2,1)S(1)}, bf16[2,4,32,512]{3,2,1,0:T(8,128)(2,1)S(1)}, u32[]{:S(2)}, u32[]{:S(2)}) collective-permute-start(bf16[2,4,32,512]{3,2,1,0:T(8,128)(2,1)S(1)} %pad_maximum_fusion), channel_id=1, source_target_pairs={{0,128},{32,160},{64,192},{96,224},{128,0},{160,32},{192,64},{224,... | collective-permute-start | bytes 786440 | tf_op jit(solution)/shard_map/ppermute | solution.py:189
  61.3 18.9 %collective-permute-start.6 = (bf16[2,4,32,512]{3,2,1,0:T(8,128)(2,1)S(1)}, bf16[2,4,32,512]{3,2,1,0:T(8,128)(2,1)S(1)}, u32[]{:S(2)}, u32[]{:S(2)}) collective-permute-start(bf16[2,4,32,512]{3,2,1,0:T(8,128)(2,1)S(1)} %pad_maximum_fusion), channel_id=1, source_target_pairs={{0,192},{32,224},{64,128},{96,160},{128,64},{160,96},{192,0},{224,... | collective-permute-start | bytes 786440 | tf_op jit(solution)/shard_map/ppermute | solution.py:189
  71.9 7.8 %collective-permute-start.13 = (bf16[2,4,32,512]{3,2,1,0:T(8,128)(2,1)S(1)}, bf16[2,4,32,512]{3,2,1,0:T(8,128)(2,1)S(1)}, u32[]{:S(2)}, u32[]{:S(2)}) collective-permute-start(bf16[2,4,32,512]{3,2,1,0:T(8,128)(2,1)S(1)} %add_add_fusion.left_a), channel_id=1, source_target_pairs={{0,2},{1,3},{2,0},{3,1},{4,6},{5,7},{6,4},{7,5},{8,10},{9,11},{10,... | collective-permute-start | bytes 786440 | tf_op jit(solution)/shard_map/ppermute | solution.py:186
  72.0 8.2 %collective-permute-start.12 = (bf16[2,4,32,512]{3,2,1,0:T(8,128)(2,1)S(1)}, bf16[2,4,32,512]{3,2,1,0:T(8,128)(2,1)S(1)}, u32[]{:S(2)}, u32[]{:S(2)}) collective-permute-start(bf16[2,4,32,512]{3,2,1,0:T(8,128)(2,1)S(1)} %add_add_fusion.left_a), channel_id=1, source_target_pairs={{0,1},{1,0},{2,3},{3,2},{4,5},{5,4},{6,7},{7,6},{8,9},{9,8},{10,11... | collective-permute-start | bytes 786440 | tf_op jit(solution)/shard_map/ppermute | solution.py:186
  79.8 1.6 %collective-permute-start.14 = (bf16[2,4,32,512]{3,2,1,0:T(8,128)(2,1)S(1)}, bf16[2,4,32,512]{3,2,1,0:T(8,128)(2,1)S(1)}, u32[]{:S(2)}, u32[]{:S(2)}) collective-permute-start(bf16[2,4,32,512]{3,2,1,0:T(8,128)(2,1)S(1)} %collective-permute-done.13.left_c), channel_id=1, source_target_pairs={{0,1},{1,0},{2,3},{3,2},{4,5},{5,4},{6,7},{7,6},{8,9},{9,8},{10,11... | collective-permute-start | bytes 786440 | tf_op jit(solution)/shard_map/ppermute | solution.py:186

commit v3 on v2

--- a/solution.py
+++ b/solution.py
@@ -13,7 +13,7 @@
 OVER_ROWS = (((0,), (0,)), ((), ()))
 
 
-def tile_kernel(orders, owners, inv_hbm, cpl_hbm, slab_hbm, send_hbm, keep, inv, cpl, slab, tiles, sems, out_sems):
+def tile_kernel(orders, owners, inv_hbm, cpl_hbm, slab_hbm, send_hbm, keep_b, keep_c, keep_d, inv, cpl, slab, slices, tiles, sems, out_sems):
     me = lax.axis_index("row")
     slab_copy = pltpu.make_async_copy(slab_hbm, slab, sems.at[8])
     cpl_copies = [pltpu.make_async_copy(cpl_hbm.at[s], cpl.at[s], sems.at[s]) for s in range(4)]
@@ -25,9 +25,11 @@
         cpl_copies[s].start()
         inv_copies[s].start()
     slab_copy.wait()
-    for y in range(4):
+    for y, keep in ((1, keep_b), (2, keep_c), (3, keep_d)):
         for b in range(4):
-            keep[y, b] = slab[b * 128 + y * 32:b * 128 + y * 32 + 32, :].astype(BF)
+            keep[b] = slab[b * 128 + y * 32:b * 128 + y * 32 + 32, :].astype(BF)
+    row = lax.broadcasted_iota(jnp.int32, (128, 128), 0)
+    col = lax.broadcasted_iota(jnp.int32, (128, 128), 1)
     copies = []
     for s in range(4):
         cpl_copies[s].wait()
@@ -35,15 +37,26 @@
         masked = jnp.where(live, cpl[s], jnp.zeros((1024, 256), BF))
         inv_copies[s].wait()
         solved = lax.dot_general(masked, inv[s], OVER_ROWS, preferred_element_type=F32).astype(BF)
-        tile = jnp.dot(solved, masked, preferred_element_type=F32).astype(BF)
+        tile = jnp.dot(solved, masked, preferred_element_type=F32)
         owner = owners[s, me]
+        second = tile[128:, 128:]
+        packed = jnp.where(row <= col, tile[:128, :128], second).astype(BF)
+        diagonal = jnp.sum(jnp.where(row == col, second, 0.0), axis=0, keepdims=True)
+        tile = tile.astype(BF)
         for k in range(8):
-            tiles[s, k // 2, k % 2, :, 0:256] = tile[k * 16:k * 16 + 16]
-            tiles[s, k // 2, k % 2, :, 256:512] = tile[128 + k * 16:144 + k * 16]
-        copy = pltpu.make_async_copy(tiles.at[s], send_hbm.at[owner // 2, owner % 2, 1:5], out_sems.at[s])
+            tiles[s, k] = packed[k * 16:k * 16 + 16]
+            tiles[s, 8 + k] = tile[k * 16:k * 16 + 16, 128:]
+        tiles[s, 16] = jnp.broadcast_to(diagonal, (16, 128)).astype(BF)
+        for half in range(2):
+            for k in range(8):
+                for side in range(2):
+                    slices[s, k // 2, half * 4 + side * 2 + k % 2] = tile[
+                        half * 128 + k * 16:half * 128 + k * 16 + 16, side * 128:side * 128 + 128
+                    ]
+        copy = pltpu.make_async_copy(tiles.at[s], send_hbm.at[owner // 2, owner % 2, 8:25], out_sems.at[s])
         copy.start()
         copies.append(copy)
-        panel_copy = pltpu.make_async_copy(tiles.at[s], send_hbm.at[:, owner % 2, 0], out_sems.at[4 + s])
+        panel_copy = pltpu.make_async_copy(slices.at[s], send_hbm.at[:, owner % 2, 0:8], out_sems.at[4 + s])
         copies.append((owner, panel_copy))
 
         @pl.when(owner < 2)
@@ -57,17 +70,18 @@
             copy.wait()
 
 
-def panel_kernel(owners, offsets, piv, got, keep, far_a, far_b, far_c, piece, left, acc, piv_cols):
+def panel_kernel(owners, offsets, piv, got, slab, far_a, far_b, far_c, piece, left, acc, piv_cols):
     me = lax.axis_index("row")
     place = me // 2
     piv_cols[...] = piv[...].T
 
     @pl.when(place == 0)
     def _():
-        acc[...] = keep[0].astype(F32)
-
-    for y, far in enumerate((far_a, far_b, far_c)):
-        @pl.when(place == y + 1)
+        for b in range(4):
+            acc[b] = slab[b * 128:b * 128 + 32, :]
+
+    for y, far in ((1, far_a), (2, far_b), (3, far_c)):
+        @pl.when(place == y)
         def _():
             acc[...] = far[...].astype(F32)
 
@@ -76,10 +90,11 @@
             @pl.when(owners[s, src] == me % 2)
             def _():
                 block = offsets[s, 0, src]
-                cols = pl.ds(pl.multiple_of(offsets[s, 1, src] * 128, 128), 256)
-                rows = got[src, 0].reshape(32, 512).astype(F32)
-                acc[block, :, cols] -= rows[:, 0:256]
-                acc[block + 1, :, cols] -= rows[:, 256:512]
+                for half in range(2):
+                    for side in range(2):
+                        cols = pl.ds(pl.multiple_of((offsets[s, 1, src] + side) * 128, 128), 128)
+                        unit = half * 4 + side * 2
+                        acc[block + half, :, cols] -= got[src, unit:unit + 2].reshape(32, 128).astype(F32)
     piece[...] = acc[...].astype(BF)
     mine = piv_cols[pl.ds(pl.multiple_of(place * 32, 32), 32), :]
     first = me % 2 == 0
@@ -100,16 +115,25 @@
 
 def base_kernel(owners, offsets, slab, tiles, out):
     me = lax.axis_index("row")
+    row = lax.broadcasted_iota(jnp.int32, (128, 128), 0)
+    col = lax.broadcasted_iota(jnp.int32, (128, 128), 1)
     out[...] = slab[...]
     for src in range(8):
         for s in range(4):
             @pl.when(owners[s, src] == me)
             def _():
-                row = pl.multiple_of(offsets[s, 0, src] * 128, 128)
-                cols = pl.ds(pl.multiple_of(offsets[s, 1, src] * 128, 128), 256)
-                block = tiles[src, 1:5].reshape(128, 512)
-                out[pl.ds(row, 128), cols] -= block[:, 0:256].astype(F32)
-                out[pl.ds(row + 128, 128), cols] -= block[:, 256:512].astype(F32)
+                top = pl.multiple_of(offsets[s, 0, src] * 128, 128)
+                start = pl.multiple_of(offsets[s, 1, src] * 128, 128)
+                upper, lower = pl.ds(top, 128), pl.ds(top + 128, 128)
+                first, second = pl.ds(start, 128), pl.ds(start + 128, 128)
+                packed = tiles[src, 8:16].reshape(128, 128).astype(F32)
+                right = tiles[src, 16:24].reshape(128, 128).astype(F32)
+                diagonal = tiles[src, 24].astype(F32)[0:1, :]
+                turned = packed.T
+                out[upper, first] -= jnp.where(row <= col, packed, turned)
+                out[upper, second] -= right
+                out[lower, first] -= right.T
+                out[lower, second] -= jnp.where(row > col, packed, jnp.where(row < col, turned, diagonal))
 
 
 def middle_kernel(base, got, left_a, left_b, left_c, out):
@@ -146,16 +170,17 @@
 def body(inverses, coupling, orders, owners, offsets, dense_slab, pivots):
     owner_rows = owners[:, :, 0].T
     offset_rows = offsets.transpose(1, 2, 0)
-    send, keep = call(
+    send, *keep = call(
         tile_kernel,
-        (shape(4, 2, 5, 2, 16, 512), shape(4, 4, 32, 512)),
+        (shape(4, 2, 25, 16, 128),) + (shape(4, 32, 512),) * 3,
         [SM, SM, HB, HB, HB],
-        (HB, VM),
+        (HB, VM, VM, VM),
         (
             pltpu.VMEM((4, 1024, 1024), BF),
             pltpu.VMEM((4, 1024, 256), BF),
             pltpu.VMEM((512, 512), F32),
-            pltpu.VMEM((4, 4, 2, 16, 512), BF),
+            pltpu.VMEM((4, 4, 8, 16, 128), BF),
+            pltpu.VMEM((4, 17, 16, 128), BF),
             pltpu.SemaphoreType.DMA((9,)),
             pltpu.SemaphoreType.DMA((8,)),
         ),
@@ -163,8 +188,8 @@
         14_000_000,
         limit=WHOLE,
     )(orders, owner_rows, inverses[0], coupling[0], dense_slab)
-    tiles = lax.all_to_all(send.reshape(8, 5, 2, 16, 512), "row", 0, 0, tiled=True)
-    far = [lax.ppermute(keep[k], "row", [(0, 2 * k), (1, 2 * k + 1)]) for k in range(1, 4)]
+    tiles = lax.all_to_all(send.reshape(8, 25, 16, 128), "row", 0, 0, tiled=True)
+    far = [lax.ppermute(keep[k - 1], "row", [(0, 2 * k), (1, 2 * k + 1)]) for k in range(1, 4)]
     piece, left = call(
         panel_kernel,
         (shape(4, 32, 512), shape(4, 32, 512)),
@@ -173,7 +198,7 @@
         (pltpu.VMEM((4, 32, 512), F32), pltpu.VMEM((128, 8), F32)),
         1_000_000,
         2_000_000,
-    )(owner_rows, offset_rows, pivots.reshape(8, 128), tiles, keep, *far)
+    )(owner_rows, offset_rows, pivots.reshape(8, 128), tiles, dense_slab, *far)
 
     def hop(mask):
         pairs = [(r * 32 + c, c * 32 + (r ^ mask) * 4 + (r & 3)) for r in range(8) for c in range(8)]

time: 83 us -> 78.8 us (0.949)
  waiting for transfers between devices: 29.2 us -> 24.3 us
  Pallas kernels: 13 us -> 13.9 us
    ppermute x3, waiting for transfers between devices: 12.1 us -> 7.38 us  [body(): lax.ppermute(keep[k - 1], 'row', [(0, 2 * k), (1, 2 * k + 1)])]
where the time goes in v3:
time: 78.8 us; the launch traced here: 78.5 us
  starting transfers between devices  39.8 us (51%)
  waiting for transfers between devices  24.3 us (31%)
  Pallas kernels  13.9 us (18%)
    ppermute x2, starting transfers between devices, hop(): return lax.ppermute(left, ROWS, pairs)  14.1 us
    pallas_call x1, Pallas kernels, body(): call(tile_kernel, (shape(4, 2, 25, 16, 128),) + (shape(4, 32, 512),) * 3,...  9.58 us
    ppermute x3, waiting for transfers between devices, spread(): lax.ppermute(value, 'col', [(z * 4 + (z & 3), (z ^ mask) * 4 + (z & 3)) f...  8.91 us
    ppermute x3, waiting for transfers between devices, over_col(): return lax.ppermute(value, 'col', [(c, c ^ mask) for c in range(32)])  7.99 us
    all_to_all x1, starting transfers between devices, body(): lax.all_to_all(send.reshape(8, 25, 16, 128), 'row', 0, 0, tiled=True)  7.49 us
    ppermute x4, starting transfers between devices, over_row(): return lax.ppermute(value, 'row', [(r, r ^ mask) for r in range(8)])  7.47 us
    ppermute x3, waiting for transfers between devices, body(): lax.ppermute(keep[k - 1], 'row', [(0, 2 * k), (1, 2 * k + 1)])  7.38 us
    ppermute x3, starting transfers between devices, body(): lax.ppermute(keep[k - 1], 'row', [(0, 2 * k), (1, 2 * k + 1)])  6.83 us
  transfers between devices with their start and end apart: 16, of which 5 were waited for; matrix products, arithmetic and copies ran while one was open for 0% of the time, Pallas kernels for 2%

profile of v3, /device:TPU:1, one launch (start us, length us, event | category | flops | bytes accessed | tf_op | source)
XLA Modules:
  0.0 78.5 jit_solution(1755995324402265507)
XLA Ops:
  0.0 9.6 %shard_map.73 = (bf16[4,2,25,16,128]{4,3,2,1,0:T(8,128)(2,1)}, bf16[4,32,512]{2,1,0:T(8,128)(2,1)}, bf16[4,32,512]{2,1,0:T(8,128)(2,1)}, bf16[4,32,512]{2,1,0:T(8,128)(2,1)}) custom-call(s32[1,4]{1,0:T(1,128)} %orders.1, s32[4,8]{1,0:T(4,128)} %bitcast.15, bf16[4,1024,1024]{2,1,0:T(8,128)(2,1)} %bitcast.21, bf16[4,1024,256]{2,1,0:T(8,128)(2,1)} %bitcast.22, ...), custom_call_target="tpu_custom_call" | custom-call | flops 2700000000 | bytes 14000000 | tf_op jit(solution)/shard_map/pallas_call | solution.py:173
  9.6 7.5 %all-to-all-start = ((bf16[8,25,16,128]{3,2,1,0:T(8,128)(2,1)}), bf16[8,25,16,128]{3,2,1,0:T(8,128)(2,1)S(1)}, u32[]{:S(2)}, u32[]{:S(2)}) async-start(bf16[8,25,16,128]{3,2,1,0:T(8,128)(2,1)} %bitcast.23), calls=%async_computation | async-start | bytes 1638400 | tf_op jit(solution)/shard_map/all_to_all | solution.py:191
  17.1 3.4 %collective-permute-start = (bf16[4,32,512]{2,1,0:T(8,128)(2,1)}, bf16[4,32,512]{2,1,0:T(8,128)(2,1)S(1)}, u32[]{:S(2)}, u32[]{:S(2)}) collective-permute-start(bf16[4,32,512]{2,1,0:T(8,128)(2,1)} %get-tuple-element.12), channel_id=1, source_target_pairs={{0,64},{32,96},{1,65},{33,97},{2,66},{34,98},{3,67},{35,99},{4,68}... | collective-permute-start | bytes 393224 | tf_op jit(solution)/shard_map/ppermute | solution.py:192
  20.5 2.2 %collective-permute-start.1 = (bf16[4,32,512]{2,1,0:T(8,128)(2,1)}, bf16[4,32,512]{2,1,0:T(8,128)(2,1)S(1)}, u32[]{:S(2)}, u32[]{:S(2)}) collective-permute-start(bf16[4,32,512]{2,1,0:T(8,128)(2,1)} %get-tuple-element.13), channel_id=1, source_target_pairs={{0,128},{32,160},{1,129},{33,161},{2,130},{34,162},{3,131},{35,163... | collective-permute-start | bytes 393224 | tf_op jit(solution)/shard_map/ppermute | solution.py:192
  22.7 1.3 %collective-permute-start.2 = (bf16[4,32,512]{2,1,0:T(8,128)(2,1)}, bf16[4,32,512]{2,1,0:T(8,128)(2,1)S(1)}, u32[]{:S(2)}, u32[]{:S(2)}) collective-permute-start(bf16[4,32,512]{2,1,0:T(8,128)(2,1)} %get-tuple-element.14), channel_id=1, source_target_pairs={{0,192},{32,224},{1,193},{33,225},{2,194},{34,226},{3,195},{35,227... | collective-permute-start | bytes 393224 | tf_op jit(solution)/shard_map/ppermute | solution.py:192
  24.0 1.8 %collective-permute-done.far_a = bf16[4,32,512]{2,1,0:T(8,128)(2,1)S(1)} collective-permute-done((bf16[4,32,512]{2,1,0:T(8,128)(2,1)}, bf16[4,32,512]{2,1,0:T(8,128)(2,1)S(1)}, u32[]{:S(2)}, u32[]{:S(2)}) %collective-permute-start) | collective-permute-done | bytes 131104 | tf_op jit(solution)/shard_map/ppermute | solution.py:192
  25.7 5.6 %collective-permute-done.1.far_b = bf16[4,32,512]{2,1,0:T(8,128)(2,1)S(1)} collective-permute-done((bf16[4,32,512]{2,1,0:T(8,128)(2,1)}, bf16[4,32,512]{2,1,0:T(8,128)(2,1)S(1)}, u32[]{:S(2)}, u32[]{:S(2)}) %collective-permute-start.1) | collective-permute-done | bytes 131104 | tf_op jit(solution)/shard_map/ppermute | solution.py:192
  31.4 1.2 %shard_map.75 = (bf16[4,32,512]{2,1,0:T(8,128)(2,1)S(1)}, bf16[4,32,512]{2,1,0:T(8,128)(2,1)S(1)}) custom-call(s32[4,8]{1,0:T(4,128)S(1)} %bitcast.16, s32[4,2,8]{2,1,0:T(2,128)S(1)} %bitcast.18, f32[8,128]{1,0:T(8,128)S(1)} %bitcast.20, bf16[8,25,16,128]{3,2,1,0:T(8,128)(2,1)S(1)} %all-to-all-done.tiles.got, f32[512,512]{1,0:T(8,128)S(1)} %copy-done, ...), custom_call_target="tpu_custom_call" | custom-call | flops 1000000 | bytes 2000000 | tf_op jit(solution)/shard_map/pallas_call | solution.py:193
  32.6 12.8 %collective-permute-start.8 = (bf16[4,32,512]{2,1,0:T(8,128)(2,1)S(1)}, bf16[4,32,512]{2,1,0:T(8,128)(2,1)S(1)}, u32[]{:S(2)}, u32[]{:S(2)}) collective-permute-start(bf16[4,32,512]{2,1,0:T(8,128)(2,1)S(1)} %get-tuple-element.16), channel_id=1, source_target_pairs={{0,16},{1,48},{2,80},{3,112},{4,144},{5,176},{6,208},{7,240},{32,2... | collective-permute-start | bytes 393224 | tf_op jit(solution)/shard_map/ppermute | solution.py:205
  45.4 1.3 %collective-permute-start.7 = (bf16[4,32,512]{2,1,0:T(8,128)(2,1)S(1)}, bf16[4,32,512]{2,1,0:T(8,128)(2,1)S(1)}, u32[]{:S(2)}, u32[]{:S(2)}) collective-permute-start(bf16[4,32,512]{2,1,0:T(8,128)(2,1)S(1)} %get-tuple-element.16), channel_id=1, source_target_pairs={{0,0},{1,32},{2,64},{3,96},{4,128},{5,160},{6,192},{7,224},{32,5},... | collective-permute-start | bytes 393224 | tf_op jit(solution)/shard_map/ppermute | solution.py:205
  46.7 3.5 %collective-permute-start.3 = (bf16[4,32,512]{2,1,0:T(8,128)(2,1)S(1)}, bf16[4,32,512]{2,1,0:T(8,128)(2,1)S(1)}, u32[]{:S(2)}, u32[]{:S(2)}) collective-permute-start(bf16[4,32,512]{2,1,0:T(8,128)(2,1)S(1)} %get-tuple-element.15), channel_id=1, source_target_pairs={{0,32},{32,0},{64,96},{96,64},{128,160},{160,128},{192,224},{224,1... | collective-permute-start | bytes 393224 | tf_op jit(solution)/shard_map/ppermute | solution.py:214
  50.3 1.2 %shard_map.74.base = f32[512,512]{1,0:T(8,128)S(1)} custom-call(s32[4,8]{1,0:T(4,128)S(1)} %bitcast.17, s32[4,2,8]{2,1,0:T(2,128)S(1)} %bitcast.19, f32[512,512]{1,0:T(8,128)S(1)} %copy-done, bf16[8,25,16,128]{3,2,1,0:T(8,128)(2,1)S(1)} %all-to-all-done.tiles.got), custom_call_target="tpu_custom_call" | custom-call | flops 1000000 | bytes 3000000 | tf_op jit(solution)/shard_map/pallas_call | solution.py:224
  51.5 0.7 collective-permute-start.10
  52.2 0.7 collective-permute-start.11
  52.9 1.3 %collective-permute-start.9 = (bf16[2,4,32,512]{3,2,1,0:T(8,128)(2,1)S(1)}, bf16[2,4,32,512]{3,2,1,0:T(8,128)(2,1)S(1)}, u32[]{:S(2)}, u32[]{:S(2)}) collective-permute-start(bf16[2,4,32,512]{3,2,1,0:T(8,128)(2,1)S(1)} %pad_maximum_fusion.1), channel_id=1, source_target_pairs={{0,4},{5,1},{10,14},{15,11},{16,20},{21,17},{26,30},{31,27},{32,36... | collective-permute-start | bytes 786440 | tf_op jit(solution)/shard_map/ppermute | solution.py:208
  54.4 2.3 %collective-permute-start.5 = (bf16[2,4,32,512]{3,2,1,0:T(8,128)(2,1)S(1)}, bf16[2,4,32,512]{3,2,1,0:T(8,128)(2,1)S(1)}, u32[]{:S(2)}, u32[]{:S(2)}) collective-permute-start(bf16[2,4,32,512]{3,2,1,0:T(8,128)(2,1)S(1)} %pad_maximum_fusion), channel_id=1, source_target_pairs={{0,128},{32,160},{64,192},{96,224},{128,0},{160,32},{192,64},{224,... | collective-permute-start | bytes 786440 | tf_op jit(solution)/shard_map/ppermute | solution.py:214
  56.7 1.5 %collective-permute-start.6 = (bf16[2,4,32,512]{3,2,1,0:T(8,128)(2,1)S(1)}, bf16[2,4,32,512]{3,2,1,0:T(8,128)(2,1)S(1)}, u32[]{:S(2)}, u32[]{:S(2)}) collective-permute-start(bf16[2,4,32,512]{3,2,1,0:T(8,128)(2,1)S(1)} %pad_maximum_fusion), channel_id=1, source_target_pairs={{0,192},{32,224},{64,128},{96,160},{128,64},{160,96},{192,0},{224,... | collective-permute-start | bytes 786440 | tf_op jit(solution)/shard_map/ppermute | solution.py:214
  58.2 8.9 %collective-permute-done.9 = bf16[2,4,32,512]{3,2,1,0:T(8,128)(2,1)S(1)} collective-permute-done((bf16[2,4,32,512]{3,2,1,0:T(8,128)(2,1)S(1)}, bf16[2,4,32,512]{3,2,1,0:T(8,128)(2,1)S(1)}, u32[]{:S(2)}, u32[]{:S(2)}) %collective-permute-start.9) | collective-permute-done | bytes 262176 | tf_op jit(solution)/shard_map/ppermute | solution.py:208
  67.3 0.7 collective-permute-start.12
  68.0 7.5 %collective-permute-done.13.left_c = bf16[2,4,32,512]{3,2,1,0:T(8,128)(2,1)S(1)} collective-permute-done((bf16[2,4,32,512]{3,2,1,0:T(8,128)(2,1)S(1)}, bf16[2,4,32,512]{3,2,1,0:T(8,128)(2,1)S(1)}, u32[]{:S(2)}, u32[]{:S(2)}) %collective-permute-start.13) | collective-permute-done | bytes 262176 | tf_op jit(solution)/shard_map/ppermute | solution.py:211
  75.5 0.5 collective-permute-start.14
  76.1 0.6 shard_map.76.so_far
  76.7 0.5 collective-permute-done.14.left
  77.2 1.3 %shard_map.77 = f32[512,512]{1,0:T(8,128)} custom-call(f32[512,512]{1,0:T(8,128)S(1)} %shard_map.76.so_far, bf16[8,4,32,512]{3,2,1,0:T(8,128)(2,1)S(1)} %constant_dynamic-update-slice_fusion.got, bf16[2,4,32,512]{3,2,1,0:T(8,128)(2,1)S(1)} %collective-permute-done.14.left), custom_call_target="tpu_custom_call" | custom-call | flops 135000000 | bytes 3000000 | tf_op jit(solution)/shard_map/pallas_call | solution.py:228
  (29 shorter events, 0.4 us)
Async XLA Ops:
  0.0 31.3 %copy-start.1 = (s32[8,4,1]{0,2,1:T(1,128)S(1)}, s32[8,4,1]{0,2,1:T(1,128)}, u32[]{:S(2)}) copy-start(s32[8,4,1]{0,2,1:T(1,128)} %param.10) | copy-start | bytes 388
  0.0 31.3 %copy-start = (f32[512,512]{1,0:T(8,128)S(1)}, f32[512,512]{1,0:T(8,128)}, u32[]{:S(2)}) copy-start(f32[512,512]{1,0:T(8,128)} %slab.3) | copy-start | bytes 3145732
  0.0 31.4 %copy-start.2 = (s32[8,4,2]{0,2,1:T(2,128)S(1)}, s32[8,4,2]{0,2,1:T(2,128)}, u32[]{:S(2)}) copy-start(s32[8,4,2]{0,2,1:T(2,128)} %param.11) | copy-start | bytes 772
  0.0 31.4 %copy-start.3 = (f32[1024]{0:T(1024)S(1)}, f32[1024]{0:T(1024)}, u32[]{:S(2)}) copy-start(f32[1024]{0:T(1024)} %param.13) | copy-start | bytes 12292
  9.6 21.7 %all-to-all-start = ((bf16[8,25,16,128]{3,2,1,0:T(8,128)(2,1)}), bf16[8,25,16,128]{3,2,1,0:T(8,128)(2,1)S(1)}, u32[]{:S(2)}, u32[]{:S(2)}) async-start(bf16[8,25,16,128]{3,2,1,0:T(8,128)(2,1)} %bitcast.23), calls=%async_computation | async-start | bytes 1638400 | tf_op jit(solution)/shard_map/all_to_all | solution.py:191
  17.1 8.6 %collective-permute-start = (bf16[4,32,512]{2,1,0:T(8,128)(2,1)}, bf16[4,32,512]{2,1,0:T(8,128)(2,1)S(1)}, u32[]{:S(2)}, u32[]{:S(2)}) collective-permute-start(bf16[4,32,512]{2,1,0:T(8,128)(2,1)} %get-tuple-element.12), channel_id=1, source_target_pairs={{0,64},{32,96},{1,65},{33,97},{2,66},{34,98},{3,67},{35,99},{4,68}... | collective-permute-start | bytes 393224 | tf_op jit(solution)/shard_map/ppermute | solution.py:192
  20.5 10.9 %collective-permute-start.1 = (bf16[4,32,512]{2,1,0:T(8,128)(2,1)}, bf16[4,32,512]{2,1,0:T(8,128)(2,1)S(1)}, u32[]{:S(2)}, u32[]{:S(2)}) collective-permute-start(bf16[4,32,512]{2,1,0:T(8,128)(2,1)} %get-tuple-element.13), channel_id=1, source_target_pairs={{0,128},{32,160},{1,129},{33,161},{2,130},{34,162},{3,131},{35,163... | collective-permute-start | bytes 393224 | tf_op jit(solution)/shard_map/ppermute | solution.py:192
  22.7 8.7 %collective-permute-start.2 = (bf16[4,32,512]{2,1,0:T(8,128)(2,1)}, bf16[4,32,512]{2,1,0:T(8,128)(2,1)S(1)}, u32[]{:S(2)}, u32[]{:S(2)}) collective-permute-start(bf16[4,32,512]{2,1,0:T(8,128)(2,1)} %get-tuple-element.14), channel_id=1, source_target_pairs={{0,192},{32,224},{1,193},{33,225},{2,194},{34,226},{3,195},{35,227... | collective-permute-start | bytes 393224 | tf_op jit(solution)/shard_map/ppermute | solution.py:192
  32.6 18.9 %collective-permute-start.8 = (bf16[4,32,512]{2,1,0:T(8,128)(2,1)S(1)}, bf16[4,32,512]{2,1,0:T(8,128)(2,1)S(1)}, u32[]{:S(2)}, u32[]{:S(2)}) collective-permute-start(bf16[4,32,512]{2,1,0:T(8,128)(2,1)S(1)} %get-tuple-element.16), channel_id=1, source_target_pairs={{0,16},{1,48},{2,80},{3,112},{4,144},{5,176},{6,208},{7,240},{32,2... | collective-permute-start | bytes 393224 | tf_op jit(solution)/shard_map/ppermute | solution.py:205
  45.4 6.1 %collective-permute-start.7 = (bf16[4,32,512]{2,1,0:T(8,128)(2,1)S(1)}, bf16[4,32,512]{2,1,0:T(8,128)(2,1)S(1)}, u32[]{:S(2)}, u32[]{:S(2)}) collective-permute-start(bf16[4,32,512]{2,1,0:T(8,128)(2,1)S(1)} %get-tuple-element.16), channel_id=1, source_target_pairs={{0,0},{1,32},{2,64},{3,96},{4,128},{5,160},{6,192},{7,224},{32,5},... | collective-permute-start | bytes 393224 | tf_op jit(solution)/shard_map/ppermute | solution.py:205
  46.7 7.5 %collective-permute-start.3 = (bf16[4,32,512]{2,1,0:T(8,128)(2,1)S(1)}, bf16[4,32,512]{2,1,0:T(8,128)(2,1)S(1)}, u32[]{:S(2)}, u32[]{:S(2)}) collective-permute-start(bf16[4,32,512]{2,1,0:T(8,128)(2,1)S(1)} %get-tuple-element.15), channel_id=1, source_target_pairs={{0,32},{32,0},{64,96},{96,64},{128,160},{160,128},{192,224},{224,1... | collective-permute-start | bytes 393224 | tf_op jit(solution)/shard_map/ppermute | solution.py:214
  51.5 5.1 %collective-permute-start.10 = (bf16[2,4,32,512]{3,2,1,0:T(8,128)(2,1)S(1)}, bf16[2,4,32,512]{3,2,1,0:T(8,128)(2,1)S(1)}, u32[]{:S(2)}, u32[]{:S(2)}) collective-permute-start(bf16[2,4,32,512]{3,2,1,0:T(8,128)(2,1)S(1)} %pad_maximum_fusion.1), channel_id=1, source_target_pairs={{0,8},{5,13},{10,2},{15,7},{16,24},{21,29},{26,18},{31,23},{32,40}... | collective-permute-start | bytes 786440 | tf_op jit(solution)/shard_map/ppermute | solution.py:208
  52.2 6.0 %collective-permute-start.11 = (bf16[2,4,32,512]{3,2,1,0:T(8,128)(2,1)S(1)}, bf16[2,4,32,512]{3,2,1,0:T(8,128)(2,1)S(1)}, u32[]{:S(2)}, u32[]{:S(2)}) collective-permute-start(bf16[2,4,32,512]{3,2,1,0:T(8,128)(2,1)S(1)} %pad_maximum_fusion.1), channel_id=1, source_target_pairs={{0,12},{5,9},{10,6},{15,3},{16,28},{21,25},{26,22},{31,19},{32,44}... | collective-permute-start | bytes 786440 | tf_op jit(solution)/shard_map/ppermute | solution.py:208
  52.9 14.2 %collective-permute-start.9 = (bf16[2,4,32,512]{3,2,1,0:T(8,128)(2,1)S(1)}, bf16[2,4,32,512]{3,2,1,0:T(8,128)(2,1)S(1)}, u32[]{:S(2)}, u32[]{:S(2)}) collective-permute-start(bf16[2,4,32,512]{3,2,1,0:T(8,128)(2,1)S(1)} %pad_maximum_fusion.1), channel_id=1, source_target_pairs={{0,4},{5,1},{10,14},{15,11},{16,20},{21,17},{26,30},{31,27},{32,36... | collective-permute-start | bytes 786440 | tf_op jit(solution)/shard_map/ppermute | solution.py:208
  54.3 13.7 %collective-permute-start.4 = (bf16[2,4,32,512]{3,2,1,0:T(8,128)(2,1)S(1)}, bf16[2,4,32,512]{3,2,1,0:T(8,128)(2,1)S(1)}, u32[]{:S(2)}, u32[]{:S(2)}) collective-permute-start(bf16[2,4,32,512]{3,2,1,0:T(8,128)(2,1)S(1)} %pad_maximum_fusion), channel_id=1, source_target_pairs={{0,64},{32,96},{64,0},{96,32},{128,192},{160,224},{192,128},{224,1... | collective-permute-start | bytes 786440 | tf_op jit(solution)/shard_map/ppermute | solution.py:214
  54.4 21.6 %collective-permute-start.5 = (bf16[2,4,32,512]{3,2,1,0:T(8,128)(2,1)S(1)}, bf16[2,4,32,512]{3,2,1,0:T(8,128)(2,1)S(1)}, u32[]{:S(2)}, u32[]{:S(2)}) collective-permute-start(bf16[2,4,32,512]{3,2,1,0:T(8,128)(2,1)S(1)} %pad_maximum_fusion), channel_id=1, source_target_pairs={{0,128},{32,160},{64,192},{96,224},{128,0},{160,32},{192,64},{224,... | collective-permute-start | bytes 786440 | tf_op jit(solution)/shard_map/ppermute | solution.py:214
  56.7 19.4 %collective-permute-start.6 = (bf16[2,4,32,512]{3,2,1,0:T(8,128)(2,1)S(1)}, bf16[2,4,32,512]{3,2,1,0:T(8,128)(2,1)S(1)}, u32[]{:S(2)}, u32[]{:S(2)}) collective-permute-start(bf16[2,4,32,512]{3,2,1,0:T(8,128)(2,1)S(1)} %pad_maximum_fusion), channel_id=1, source_target_pairs={{0,192},{32,224},{64,128},{96,160},{128,64},{160,96},{192,0},{224,... | collective-permute-start | bytes 786440 | tf_op jit(solution)/shard_map/ppermute | solution.py:214
  67.2 8.3 %collective-permute-start.13 = (bf16[2,4,32,512]{3,2,1,0:T(8,128)(2,1)S(1)}, bf16[2,4,32,512]{3,2,1,0:T(8,128)(2,1)S(1)}, u32[]{:S(2)}, u32[]{:S(2)}) collective-permute-start(bf16[2,4,32,512]{3,2,1,0:T(8,128)(2,1)S(1)} %add_add_fusion.left_a), channel_id=1, source_target_pairs={{0,2},{1,3},{2,0},{3,1},{4,6},{5,7},{6,4},{7,5},{8,10},{9,11},{10,... | collective-permute-start | bytes 786440 | tf_op jit(solution)/shard_map/ppermute | solution.py:211
  67.3 8.8 %collective-permute-start.12 = (bf16[2,4,32,512]{3,2,1,0:T(8,128)(2,1)S(1)}, bf16[2,4,32,512]{3,2,1,0:T(8,128)(2,1)S(1)}, u32[]{:S(2)}, u32[]{:S(2)}) collective-permute-start(bf16[2,4,32,512]{3,2,1,0:T(8,128)(2,1)S(1)} %add_add_fusion.left_a), channel_id=1, source_target_pairs={{0,1},{1,0},{2,3},{3,2},{4,5},{5,4},{6,7},{7,6},{8,9},{9,8},{10,11... | collective-permute-start | bytes 786440 | tf_op jit(solution)/shard_map/ppermute | solution.py:211
  75.5 1.7 %collective-permute-start.14 = (bf16[2,4,32,512]{3,2,1,0:T(8,128)(2,1)S(1)}, bf16[2,4,32,512]{3,2,1,0:T(8,128)(2,1)S(1)}, u32[]{:S(2)}, u32[]{:S(2)}) collective-permute-start(bf16[2,4,32,512]{3,2,1,0:T(8,128)(2,1)S(1)} %collective-permute-done.13.left_c), channel_id=1, source_target_pairs={{0,1},{1,0},{2,3},{3,2},{4,5},{5,4},{6,7},{7,6},{8,9},{9,8},{10,11... | collective-permute-start | bytes 786440 | tf_op jit(solution)/shard_map/ppermute | solution.py:211

commit v4 on v3

--- a/solution.py
+++ b/solution.py
@@ -20,14 +20,10 @@
     inv_copies = [pltpu.make_async_copy(inv_hbm.at[s], inv.at[s], sems.at[4 + s]) for s in range(4)]
     cpl_copies[0].start()
     inv_copies[0].start()
-    slab_copy.start()
     for s in range(1, 4):
         cpl_copies[s].start()
         inv_copies[s].start()
-    slab_copy.wait()
-    for y, keep in ((1, keep_b), (2, keep_c), (3, keep_d)):
-        for b in range(4):
-            keep[b] = slab[b * 128 + y * 32:b * 128 + y * 32 + 32, :].astype(BF)
+    slab_copy.start()
     row = lax.broadcasted_iota(jnp.int32, (128, 128), 0)
     col = lax.broadcasted_iota(jnp.int32, (128, 128), 1)
     copies = []
@@ -63,6 +59,10 @@
         def _():
             panel_copy.start()
 
+    slab_copy.wait()
+    for y, keep in ((1, keep_b), (2, keep_c), (3, keep_d)):
+        for b in range(4):
+            keep[b] = slab[b * 128 + y * 32:b * 128 + y * 32 + 32, :].astype(BF)
     for copy in copies:
         if isinstance(copy, tuple):
             pl.when(copy[0] < 2)(copy[1].wait)

time: 78.8 us -> 77.6 us (0.985)
  Pallas kernels: 13.9 us -> 12.9 us
    pallas_call x1, Pallas kernels: 9.58 us -> 8.44 us  [body(): call(tile_kernel, (shape(4, 2, 25, 16, 128),) + (shape(4, 32, 512),) * 3,...]
  transfers between devices with their start and end apart: 16 -> 16, of which waited for: 5 -> 5; matrix products, arithmetic and copies ran while one was open for 0% -> 0% of each run, Pallas kernels for 2% -> 3%
where the time goes in v4:
time: 77.6 us; the launch traced here: 77.3 us
  starting transfers between devices  39.6 us (51%)
  waiting for transfers between devices  24.3 us (31%)
  Pallas kernels  12.9 us (17%)
    ppermute x2, starting transfers between devices, hop(): return lax.ppermute(left, ROWS, pairs)  14.1 us
    ppermute x3, waiting for transfers between devices, spread(): lax.ppermute(value, 'col', [(z * 4 + (z & 3), (z ^ mask) * 4 + (z & 3)) f...  8.78 us
    pallas_call x1, Pallas kernels, body(): call(tile_kernel, (shape(4, 2, 25, 16, 128),) + (shape(4, 32, 512),) * 3,...  8.44 us
    ppermute x3, waiting for transfers between devices, over_col(): return lax.ppermute(value, 'col', [(c, c ^ mask) for c in range(32)])  8.17 us
    all_to_all x1, starting transfers between devices, body(): lax.all_to_all(send.reshape(8, 25, 16, 128), 'row', 0, 0, tiled=True)  7.54 us
    ppermute x4, starting transfers between devices, over_row(): return lax.ppermute(value, 'row', [(r, r ^ mask) for r in range(8)])  7.49 us
    ppermute x3, waiting for transfers between devices, body(): lax.ppermute(keep[k - 1], 'row', [(0, 2 * k), (1, 2 * k + 1)])  7.38 us
    ppermute x3, starting transfers between devices, body(): lax.ppermute(keep[k - 1], 'row', [(0, 2 * k), (1, 2 * k + 1)])  6.83 us
  transfers between devices with their start and end apart: 16, of which 5 were waited for; matrix products, arithmetic and copies ran while one was open for 0% of the time, Pallas kernels for 3%

profile of v4, /device:TPU:1, one launch (start us, length us, event | category | flops | bytes accessed | tf_op | source)
XLA Modules:
  0.0 77.3 jit_solution(3056797633319167724)
XLA Ops:
  0.0 8.4 %shard_map.73 = (bf16[4,2,25,16,128]{4,3,2,1,0:T(8,128)(2,1)}, bf16[4,32,512]{2,1,0:T(8,128)(2,1)}, bf16[4,32,512]{2,1,0:T(8,128)(2,1)}, bf16[4,32,512]{2,1,0:T(8,128)(2,1)}) custom-call(s32[1,4]{1,0:T(1,128)} %orders.1, s32[4,8]{1,0:T(4,128)} %bitcast.15, bf16[4,1024,1024]{2,1,0:T(8,128)(2,1)} %bitcast.21, bf16[4,1024,256]{2,1,0:T(8,128)(2,1)} %bitcast.22, ...), custom_call_target="tpu_custom_call" | custom-call | flops 2700000000 | bytes 14000000 | tf_op jit(solution)/shard_map/pallas_call | solution.py:173
  8.5 7.5 %all-to-all-start = ((bf16[8,25,16,128]{3,2,1,0:T(8,128)(2,1)}), bf16[8,25,16,128]{3,2,1,0:T(8,128)(2,1)S(1)}, u32[]{:S(2)}, u32[]{:S(2)}) async-start(bf16[8,25,16,128]{3,2,1,0:T(8,128)(2,1)} %bitcast.23), calls=%async_computation | async-start | bytes 1638400 | tf_op jit(solution)/shard_map/all_to_all | solution.py:191
  16.0 3.4 %collective-permute-start = (bf16[4,32,512]{2,1,0:T(8,128)(2,1)}, bf16[4,32,512]{2,1,0:T(8,128)(2,1)S(1)}, u32[]{:S(2)}, u32[]{:S(2)}) collective-permute-start(bf16[4,32,512]{2,1,0:T(8,128)(2,1)} %get-tuple-element.12), channel_id=1, source_target_pairs={{0,64},{32,96},{1,65},{33,97},{2,66},{34,98},{3,67},{35,99},{4,68}... | collective-permute-start | bytes 393224 | tf_op jit(solution)/shard_map/ppermute | solution.py:192
  19.4 2.2 %collective-permute-start.1 = (bf16[4,32,512]{2,1,0:T(8,128)(2,1)}, bf16[4,32,512]{2,1,0:T(8,128)(2,1)S(1)}, u32[]{:S(2)}, u32[]{:S(2)}) collective-permute-start(bf16[4,32,512]{2,1,0:T(8,128)(2,1)} %get-tuple-element.13), channel_id=1, source_target_pairs={{0,128},{32,160},{1,129},{33,161},{2,130},{34,162},{3,131},{35,163... | collective-permute-start | bytes 393224 | tf_op jit(solution)/shard_map/ppermute | solution.py:192
  21.6 1.3 %collective-permute-start.2 = (bf16[4,32,512]{2,1,0:T(8,128)(2,1)}, bf16[4,32,512]{2,1,0:T(8,128)(2,1)S(1)}, u32[]{:S(2)}, u32[]{:S(2)}) collective-permute-start(bf16[4,32,512]{2,1,0:T(8,128)(2,1)} %get-tuple-element.14), channel_id=1, source_target_pairs={{0,192},{32,224},{1,193},{33,225},{2,194},{34,226},{3,195},{35,227... | collective-permute-start | bytes 393224 | tf_op jit(solution)/shard_map/ppermute | solution.py:192
  22.9 1.8 %collective-permute-done.far_a = bf16[4,32,512]{2,1,0:T(8,128)(2,1)S(1)} collective-permute-done((bf16[4,32,512]{2,1,0:T(8,128)(2,1)}, bf16[4,32,512]{2,1,0:T(8,128)(2,1)S(1)}, u32[]{:S(2)}, u32[]{:S(2)}) %collective-permute-start) | collective-permute-done | bytes 131104 | tf_op jit(solution)/shard_map/ppermute | solution.py:192
  24.7 5.6 %collective-permute-done.1.far_b = bf16[4,32,512]{2,1,0:T(8,128)(2,1)S(1)} collective-permute-done((bf16[4,32,512]{2,1,0:T(8,128)(2,1)}, bf16[4,32,512]{2,1,0:T(8,128)(2,1)S(1)}, u32[]{:S(2)}, u32[]{:S(2)}) %collective-permute-start.1) | collective-permute-done | bytes 131104 | tf_op jit(solution)/shard_map/ppermute | solution.py:192
  30.3 1.2 %shard_map.75 = (bf16[4,32,512]{2,1,0:T(8,128)(2,1)S(1)}, bf16[4,32,512]{2,1,0:T(8,128)(2,1)S(1)}) custom-call(s32[4,8]{1,0:T(4,128)S(1)} %bitcast.16, s32[4,2,8]{2,1,0:T(2,128)S(1)} %bitcast.18, f32[8,128]{1,0:T(8,128)S(1)} %bitcast.20, bf16[8,25,16,128]{3,2,1,0:T(8,128)(2,1)S(1)} %all-to-all-done.tiles.got, f32[512,512]{1,0:T(8,128)S(1)} %copy-done, ...), custom_call_target="tpu_custom_call" | custom-call | flops 1000000 | bytes 2000000 | tf_op jit(solution)/shard_map/pallas_call | solution.py:193
  31.5 12.8 %collective-permute-start.8 = (bf16[4,32,512]{2,1,0:T(8,128)(2,1)S(1)}, bf16[4,32,512]{2,1,0:T(8,128)(2,1)S(1)}, u32[]{:S(2)}, u32[]{:S(2)}) collective-permute-start(bf16[4,32,512]{2,1,0:T(8,128)(2,1)S(1)} %get-tuple-element.16), channel_id=1, source_target_pairs={{0,16},{1,48},{2,80},{3,112},{4,144},{5,176},{6,208},{7,240},{32,2... | collective-permute-start | bytes 393224 | tf_op jit(solution)/shard_map/ppermute | solution.py:205
  44.3 1.3 %collective-permute-start.7 = (bf16[4,32,512]{2,1,0:T(8,128)(2,1)S(1)}, bf16[4,32,512]{2,1,0:T(8,128)(2,1)S(1)}, u32[]{:S(2)}, u32[]{:S(2)}) collective-permute-start(bf16[4,32,512]{2,1,0:T(8,128)(2,1)S(1)} %get-tuple-element.16), channel_id=1, source_target_pairs={{0,0},{1,32},{2,64},{3,96},{4,128},{5,160},{6,192},{7,224},{32,5},... | collective-permute-start | bytes 393224 | tf_op jit(solution)/shard_map/ppermute | solution.py:205
  45.6 3.6 %collective-permute-start.3 = (bf16[4,32,512]{2,1,0:T(8,128)(2,1)S(1)}, bf16[4,32,512]{2,1,0:T(8,128)(2,1)S(1)}, u32[]{:S(2)}, u32[]{:S(2)}) collective-permute-start(bf16[4,32,512]{2,1,0:T(8,128)(2,1)S(1)} %get-tuple-element.15), channel_id=1, source_target_pairs={{0,32},{32,0},{64,96},{96,64},{128,160},{160,128},{192,224},{224,1... | collective-permute-start | bytes 393224 | tf_op jit(solution)/shard_map/ppermute | solution.py:214
  49.2 1.4 %shard_map.74.base = f32[512,512]{1,0:T(8,128)S(1)} custom-call(s32[4,8]{1,0:T(4,128)S(1)} %bitcast.17, s32[4,2,8]{2,1,0:T(2,128)S(1)} %bitcast.19, f32[512,512]{1,0:T(8,128)S(1)} %copy-done, bf16[8,25,16,128]{3,2,1,0:T(8,128)(2,1)S(1)} %all-to-all-done.tiles.got), custom_call_target="tpu_custom_call" | custom-call | flops 1000000 | bytes 3000000 | tf_op jit(solution)/shard_map/pallas_call | solution.py:224
  50.6 0.7 collective-permute-start.10
  51.3 0.7 collective-permute-start.11
  52.0 1.3 %collective-permute-start.9 = (bf16[2,4,32,512]{3,2,1,0:T(8,128)(2,1)S(1)}, bf16[2,4,32,512]{3,2,1,0:T(8,128)(2,1)S(1)}, u32[]{:S(2)}, u32[]{:S(2)}) collective-permute-start(bf16[2,4,32,512]{3,2,1,0:T(8,128)(2,1)S(1)} %pad_maximum_fusion.1), channel_id=1, source_target_pairs={{0,4},{5,1},{10,14},{15,11},{16,20},{21,17},{26,30},{31,27},{32,36... | collective-permute-start | bytes 786440 | tf_op jit(solution)/shard_map/ppermute | solution.py:208
  53.4 2.1 %collective-permute-start.5 = (bf16[2,4,32,512]{3,2,1,0:T(8,128)(2,1)S(1)}, bf16[2,4,32,512]{3,2,1,0:T(8,128)(2,1)S(1)}, u32[]{:S(2)}, u32[]{:S(2)}) collective-permute-start(bf16[2,4,32,512]{3,2,1,0:T(8,128)(2,1)S(1)} %pad_maximum_fusion), channel_id=1, source_target_pairs={{0,128},{32,160},{64,192},{96,224},{128,0},{160,32},{192,64},{224,... | collective-permute-start | bytes 786440 | tf_op jit(solution)/shard_map/ppermute | solution.py:214
  55.5 1.7 %collective-permute-start.6 = (bf16[2,4,32,512]{3,2,1,0:T(8,128)(2,1)S(1)}, bf16[2,4,32,512]{3,2,1,0:T(8,128)(2,1)S(1)}, u32[]{:S(2)}, u32[]{:S(2)}) collective-permute-start(bf16[2,4,32,512]{3,2,1,0:T(8,128)(2,1)S(1)} %pad_maximum_fusion), channel_id=1, source_target_pairs={{0,192},{32,224},{64,128},{96,160},{128,64},{160,96},{192,0},{224,... | collective-permute-start | bytes 786440 | tf_op jit(solution)/shard_map/ppermute | solution.py:214
  57.3 8.8 %collective-permute-done.9 = bf16[2,4,32,512]{3,2,1,0:T(8,128)(2,1)S(1)} collective-permute-done((bf16[2,4,32,512]{3,2,1,0:T(8,128)(2,1)S(1)}, bf16[2,4,32,512]{3,2,1,0:T(8,128)(2,1)S(1)}, u32[]{:S(2)}, u32[]{:S(2)}) %collective-permute-start.9) | collective-permute-done | bytes 262176 | tf_op jit(solution)/shard_map/ppermute | solution.py:208
  66.2 0.5 collective-permute-start.12
  66.7 7.7 %collective-permute-done.13.left_c = bf16[2,4,32,512]{3,2,1,0:T(8,128)(2,1)S(1)} collective-permute-done((bf16[2,4,32,512]{3,2,1,0:T(8,128)(2,1)S(1)}, bf16[2,4,32,512]{3,2,1,0:T(8,128)(2,1)S(1)}, u32[]{:S(2)}, u32[]{:S(2)}) %collective-permute-start.13) | collective-permute-done | bytes 262176 | tf_op jit(solution)/shard_map/ppermute | solution.py:211
  74.4 0.4 collective-permute-start.14
  74.9 0.6 shard_map.76.so_far
  75.5 0.5 collective-permute-done.14.left
  76.0 1.3 %shard_map.77 = f32[512,512]{1,0:T(8,128)} custom-call(f32[512,512]{1,0:T(8,128)S(1)} %shard_map.76.so_far, bf16[8,4,32,512]{3,2,1,0:T(8,128)(2,1)S(1)} %constant_dynamic-update-slice_fusion.got, bf16[2,4,32,512]{3,2,1,0:T(8,128)(2,1)S(1)} %collective-permute-done.14.left), custom_call_target="tpu_custom_call" | custom-call | flops 135000000 | bytes 3000000 | tf_op jit(solution)/shard_map/pallas_call | solution.py:228
  (29 shorter events, 0.4 us)
Async XLA Ops:
  0.0 30.2 %copy-start.1 = (s32[8,4,1]{0,2,1:T(1,128)S(1)}, s32[8,4,1]{0,2,1:T(1,128)}, u32[]{:S(2)}) copy-start(s32[8,4,1]{0,2,1:T(1,128)} %param.10) | copy-start | bytes 388
  0.0 30.2 %copy-start = (f32[512,512]{1,0:T(8,128)S(1)}, f32[512,512]{1,0:T(8,128)}, u32[]{:S(2)}) copy-start(f32[512,512]{1,0:T(8,128)} %slab.3) | copy-start | bytes 3145732
  0.0 30.3 %copy-start.2 = (s32[8,4,2]{0,2,1:T(2,128)S(1)}, s32[8,4,2]{0,2,1:T(2,128)}, u32[]{:S(2)}) copy-start(s32[8,4,2]{0,2,1:T(2,128)} %param.11) | copy-start | bytes 772
  0.0 30.3 %copy-start.3 = (f32[1024]{0:T(1024)S(1)}, f32[1024]{0:T(1024)}, u32[]{:S(2)}) copy-start(f32[1024]{0:T(1024)} %param.13) | copy-start | bytes 12292
  8.5 21.8 %all-to-all-start = ((bf16[8,25,16,128]{3,2,1,0:T(8,128)(2,1)}), bf16[8,25,16,128]{3,2,1,0:T(8,128)(2,1)S(1)}, u32[]{:S(2)}, u32[]{:S(2)}) async-start(bf16[8,25,16,128]{3,2,1,0:T(8,128)(2,1)} %bitcast.23), calls=%async_computation | async-start | bytes 1638400 | tf_op jit(solution)/shard_map/all_to_all | solution.py:191
  16.0 8.7 %collective-permute-start = (bf16[4,32,512]{2,1,0:T(8,128)(2,1)}, bf16[4,32,512]{2,1,0:T(8,128)(2,1)S(1)}, u32[]{:S(2)}, u32[]{:S(2)}) collective-permute-start(bf16[4,32,512]{2,1,0:T(8,128)(2,1)} %get-tuple-element.12), channel_id=1, source_target_pairs={{0,64},{32,96},{1,65},{33,97},{2,66},{34,98},{3,67},{35,99},{4,68}... | collective-permute-start | bytes 393224 | tf_op jit(solution)/shard_map/ppermute | solution.py:192
  19.4 10.9 %collective-permute-start.1 = (bf16[4,32,512]{2,1,0:T(8,128)(2,1)}, bf16[4,32,512]{2,1,0:T(8,128)(2,1)S(1)}, u32[]{:S(2)}, u32[]{:S(2)}) collective-permute-start(bf16[4,32,512]{2,1,0:T(8,128)(2,1)} %get-tuple-element.13), channel_id=1, source_target_pairs={{0,128},{32,160},{1,129},{33,161},{2,130},{34,162},{3,131},{35,163... | collective-permute-start | bytes 393224 | tf_op jit(solution)/shard_map/ppermute | solution.py:192
  21.6 8.7 %collective-permute-start.2 = (bf16[4,32,512]{2,1,0:T(8,128)(2,1)}, bf16[4,32,512]{2,1,0:T(8,128)(2,1)S(1)}, u32[]{:S(2)}, u32[]{:S(2)}) collective-permute-start(bf16[4,32,512]{2,1,0:T(8,128)(2,1)} %get-tuple-element.14), channel_id=1, source_target_pairs={{0,192},{32,224},{1,193},{33,225},{2,194},{34,226},{3,195},{35,227... | collective-permute-start | bytes 393224 | tf_op jit(solution)/shard_map/ppermute | solution.py:192
  31.5 19.0 %collective-permute-start.8 = (bf16[4,32,512]{2,1,0:T(8,128)(2,1)S(1)}, bf16[4,32,512]{2,1,0:T(8,128)(2,1)S(1)}, u32[]{:S(2)}, u32[]{:S(2)}) collective-permute-start(bf16[4,32,512]{2,1,0:T(8,128)(2,1)S(1)} %get-tuple-element.16), channel_id=1, source_target_pairs={{0,16},{1,48},{2,80},{3,112},{4,144},{5,176},{6,208},{7,240},{32,2... | collective-permute-start | bytes 393224 | tf_op jit(solution)/shard_map/ppermute | solution.py:205
  44.3 6.2 %collective-permute-start.7 = (bf16[4,32,512]{2,1,0:T(8,128)(2,1)S(1)}, bf16[4,32,512]{2,1,0:T(8,128)(2,1)S(1)}, u32[]{:S(2)}, u32[]{:S(2)}) collective-permute-start(bf16[4,32,512]{2,1,0:T(8,128)(2,1)S(1)} %get-tuple-element.16), channel_id=1, source_target_pairs={{0,0},{1,32},{2,64},{3,96},{4,128},{5,160},{6,192},{7,224},{32,5},... | collective-permute-start | bytes 393224 | tf_op jit(solution)/shard_map/ppermute | solution.py:205
  45.6 7.7 %collective-permute-start.3 = (bf16[4,32,512]{2,1,0:T(8,128)(2,1)S(1)}, bf16[4,32,512]{2,1,0:T(8,128)(2,1)S(1)}, u32[]{:S(2)}, u32[]{:S(2)}) collective-permute-start(bf16[4,32,512]{2,1,0:T(8,128)(2,1)S(1)} %get-tuple-element.15), channel_id=1, source_target_pairs={{0,32},{32,0},{64,96},{96,64},{128,160},{160,128},{192,224},{224,1... | collective-permute-start | bytes 393224 | tf_op jit(solution)/shard_map/ppermute | solution.py:214
  50.6 4.9 %collective-permute-start.10 = (bf16[2,4,32,512]{3,2,1,0:T(8,128)(2,1)S(1)}, bf16[2,4,32,512]{3,2,1,0:T(8,128)(2,1)S(1)}, u32[]{:S(2)}, u32[]{:S(2)}) collective-permute-start(bf16[2,4,32,512]{3,2,1,0:T(8,128)(2,1)S(1)} %pad_maximum_fusion.1), channel_id=1, source_target_pairs={{0,8},{5,13},{10,2},{15,7},{16,24},{21,29},{26,18},{31,23},{32,40}... | collective-permute-start | bytes 786440 | tf_op jit(solution)/shard_map/ppermute | solution.py:208
  51.3 6.0 %collective-permute-start.11 = (bf16[2,4,32,512]{3,2,1,0:T(8,128)(2,1)S(1)}, bf16[2,4,32,512]{3,2,1,0:T(8,128)(2,1)S(1)}, u32[]{:S(2)}, u32[]{:S(2)}) collective-permute-start(bf16[2,4,32,512]{3,2,1,0:T(8,128)(2,1)S(1)} %pad_maximum_fusion.1), channel_id=1, source_target_pairs={{0,12},{5,9},{10,6},{15,3},{16,28},{21,25},{26,22},{31,19},{32,44}... | collective-permute-start | bytes 786440 | tf_op jit(solution)/shard_map/ppermute | solution.py:208
  52.0 14.1 %collective-permute-start.9 = (bf16[2,4,32,512]{3,2,1,0:T(8,128)(2,1)S(1)}, bf16[2,4,32,512]{3,2,1,0:T(8,128)(2,1)S(1)}, u32[]{:S(2)}, u32[]{:S(2)}) collective-permute-start(bf16[2,4,32,512]{3,2,1,0:T(8,128)(2,1)S(1)} %pad_maximum_fusion.1), channel_id=1, source_target_pairs={{0,4},{5,1},{10,14},{15,11},{16,20},{21,17},{26,30},{31,27},{32,36... | collective-permute-start | bytes 786440 | tf_op jit(solution)/shard_map/ppermute | solution.py:208
  53.3 13.4 %collective-permute-start.4 = (bf16[2,4,32,512]{3,2,1,0:T(8,128)(2,1)S(1)}, bf16[2,4,32,512]{3,2,1,0:T(8,128)(2,1)S(1)}, u32[]{:S(2)}, u32[]{:S(2)}) collective-permute-start(bf16[2,4,32,512]{3,2,1,0:T(8,128)(2,1)S(1)} %pad_maximum_fusion), channel_id=1, source_target_pairs={{0,64},{32,96},{64,0},{96,32},{128,192},{160,224},{192,128},{224,1... | collective-permute-start | bytes 786440 | tf_op jit(solution)/shard_map/ppermute | solution.py:214
  53.4 21.4 %collective-permute-start.5 = (bf16[2,4,32,512]{3,2,1,0:T(8,128)(2,1)S(1)}, bf16[2,4,32,512]{3,2,1,0:T(8,128)(2,1)S(1)}, u32[]{:S(2)}, u32[]{:S(2)}) collective-permute-start(bf16[2,4,32,512]{3,2,1,0:T(8,128)(2,1)S(1)} %pad_maximum_fusion), channel_id=1, source_target_pairs={{0,128},{32,160},{64,192},{96,224},{128,0},{160,32},{192,64},{224,... | collective-permute-start | bytes 786440 | tf_op jit(solution)/shard_map/ppermute | solution.py:214
  55.5 19.3 %collective-permute-start.6 = (bf16[2,4,32,512]{3,2,1,0:T(8,128)(2,1)S(1)}, bf16[2,4,32,512]{3,2,1,0:T(8,128)(2,1)S(1)}, u32[]{:S(2)}, u32[]{:S(2)}) collective-permute-start(bf16[2,4,32,512]{3,2,1,0:T(8,128)(2,1)S(1)} %pad_maximum_fusion), channel_id=1, source_target_pairs={{0,192},{32,224},{64,128},{96,160},{128,64},{160,96},{192,0},{224,... | collective-permute-start | bytes 786440 | tf_op jit(solution)/shard_map/ppermute | solution.py:214
  66.1 8.3 %collective-permute-start.13 = (bf16[2,4,32,512]{3,2,1,0:T(8,128)(2,1)S(1)}, bf16[2,4,32,512]{3,2,1,0:T(8,128)(2,1)S(1)}, u32[]{:S(2)}, u32[]{:S(2)}) collective-permute-start(bf16[2,4,32,512]{3,2,1,0:T(8,128)(2,1)S(1)} %add_add_fusion.left_a), channel_id=1, source_target_pairs={{0,2},{1,3},{2,0},{3,1},{4,6},{5,7},{6,4},{7,5},{8,10},{9,11},{10,... | collective-permute-start | bytes 786440 | tf_op jit(solution)/shard_map/ppermute | solution.py:211
  66.2 8.6 %collective-permute-start.12 = (bf16[2,4,32,512]{3,2,1,0:T(8,128)(2,1)S(1)}, bf16[2,4,32,512]{3,2,1,0:T(8,128)(2,1)S(1)}, u32[]{:S(2)}, u32[]{:S(2)}) collective-permute-start(bf16[2,4,32,512]{3,2,1,0:T(8,128)(2,1)S(1)} %add_add_fusion.left_a), channel_id=1, source_target_pairs={{0,1},{1,0},{2,3},{3,2},{4,5},{5,4},{6,7},{7,6},{8,9},{9,8},{10,11... | collective-permute-start | bytes 786440 | tf_op jit(solution)/shard_map/ppermute | solution.py:211
  74.4 1.6 %collective-permute-start.14 = (bf16[2,4,32,512]{3,2,1,0:T(8,128)(2,1)S(1)}, bf16[2,4,32,512]{3,2,1,0:T(8,128)(2,1)S(1)}, u32[]{:S(2)}, u32[]{:S(2)}) collective-permute-start(bf16[2,4,32,512]{3,2,1,0:T(8,128)(2,1)S(1)} %collective-permute-done.13.left_c), channel_id=1, source_target_pairs={{0,1},{1,0},{2,3},{3,2},{4,5},{5,4},{6,7},{7,6},{8,9},{9,8},{10,11... | collective-permute-start | bytes 786440 | tf_op jit(solution)/shard_map/ppermute | solution.py:211

commit v5 on v4

--- a/solution.py
+++ b/solution.py
@@ -109,7 +109,7 @@
     row = ((col // 4) & 4) | ((col & 3) ^ mask)
     right = jnp.concatenate([panel[row ^ me].reshape(128, 512), panel[row ^ me ^ 4].reshape(128, 512)], axis=0)
     return total - lax.dot_general(
-        left[...].reshape(256, 512), right, OVER_ROWS, preferred_element_type=F32
+        left[...].reshape(256, left.shape[-1]), right, OVER_ROWS, preferred_element_type=F32
     )
 
 
@@ -141,8 +141,15 @@
     out[...] = take(take(total, left_b, got, 1), left_c, got, 2)
 
 
-def last_kernel(so_far, got, left, out):
-    out[...] = take(so_far[...], left, got, 3)
+def last_kernel(so_far, panel, left, out_hbm, total, sems):
+    copies = []
+    for part in range(4):
+        rows = slice(part * 128, part * 128 + 128)
+        total[rows] = take(so_far[rows], left[:, :, :, rows], panel, 3)
+        copies.append(pltpu.make_async_copy(total.at[rows], out_hbm.at[rows], sems.at[part]))
+        copies[-1].start()
+    for copy in copies:
+        copy.wait()
 
 
 def call(kernel, out_shape, in_specs, out_specs, scratch=(), flops=0, nbytes=0, aliases=None, limit=LIMIT):
@@ -225,7 +232,8 @@
         owner_rows, offset_rows, dense_slab, tiles
     )
     total = call(middle_kernel, full, [VM] * 5, VM, (), 400_000_000, 4_000_000)(base, got, left_a, left_b, left_c)
-    return call(last_kernel, full, [VM] * 3, VM, (), 135_000_000, 3_000_000)(total, got, left_d)
+    parts = (pltpu.VMEM((512, 512), F32), pltpu.SemaphoreType.DMA((4,)))
+    return call(last_kernel, full, [VM] * 3, HB, parts, 135_000_000, 3_000_000)(total, got, left_d)
 
 
 def solution(mesh):

time: 77.6 us -> 77.6 us (level)
  no operation moved by 1% of the time
where the time goes in v5:
time: 77.6 us; the launch traced here: 77.2 us
  starting transfers between devices  39.9 us (51%)
  waiting for transfers between devices  24 us (31%)
  Pallas kernels  12.9 us (17%)
    ppermute x2, starting transfers between devices, hop(): return lax.ppermute(left, ROWS, pairs)  14.1 us
    ppermute x3, waiting for transfers between devices, spread(): lax.ppermute(value, 'col', [(z * 4 + (z & 3), (z ^ mask) * 4 + (z & 3)) f...  8.77 us
    pallas_call x1, Pallas kernels, body(): call(tile_kernel, (shape(4, 2, 25, 16, 128),) + (shape(4, 32, 512),) * 3,...  8.48 us
    ppermute x3, waiting for transfers between devices, over_col(): return lax.ppermute(value, 'col', [(c, c ^ mask) for c in range(32)])  7.85 us
    ppermute x4, starting transfers between devices, over_row(): return lax.ppermute(value, 'row', [(r, r ^ mask) for r in range(8)])  7.47 us
    all_to_all x1, starting transfers between devices, body(): lax.all_to_all(send.reshape(8, 25, 16, 128), 'row', 0, 0, tiled=True)  7.44 us
    ppermute x3, waiting for transfers between devices, body(): lax.ppermute(keep[k - 1], 'row', [(0, 2 * k), (1, 2 * k + 1)])  7.38 us
    ppermute x3, starting transfers between devices, body(): lax.ppermute(keep[k - 1], 'row', [(0, 2 * k), (1, 2 * k + 1)])  6.83 us
  transfers between devices with their start and end apart: 16, of which 5 were waited for; matrix products, arithmetic and copies ran while one was open for 0% of the time, Pallas kernels for 3%

profile of v5, /device:TPU:1, one launch (start us, length us, event | category | flops | bytes accessed | tf_op | source)
XLA Modules:
  0.0 77.2 jit_solution(3088648219625546689)
XLA Ops:
  0.0 8.5 %shard_map.73 = (bf16[4,2,25,16,128]{4,3,2,1,0:T(8,128)(2,1)}, bf16[4,32,512]{2,1,0:T(8,128)(2,1)}, bf16[4,32,512]{2,1,0:T(8,128)(2,1)}, bf16[4,32,512]{2,1,0:T(8,128)(2,1)}) custom-call(s32[1,4]{1,0:T(1,128)} %orders.1, s32[4,8]{1,0:T(4,128)} %bitcast.15, bf16[4,1024,1024]{2,1,0:T(8,128)(2,1)} %bitcast.21, bf16[4,1024,256]{2,1,0:T(8,128)(2,1)} %bitcast.22, ...), custom_call_target="tpu_custom_call" | custom-call | flops 2700000000 | bytes 14000000 | tf_op jit(solution)/shard_map/pallas_call | solution.py:180
  8.5 7.4 %all-to-all-start = ((bf16[8,25,16,128]{3,2,1,0:T(8,128)(2,1)}), bf16[8,25,16,128]{3,2,1,0:T(8,128)(2,1)S(1)}, u32[]{:S(2)}, u32[]{:S(2)}) async-start(bf16[8,25,16,128]{3,2,1,0:T(8,128)(2,1)} %bitcast.23), calls=%async_computation | async-start | bytes 1638400 | tf_op jit(solution)/shard_map/all_to_all | solution.py:198
  16.0 3.4 %collective-permute-start = (bf16[4,32,512]{2,1,0:T(8,128)(2,1)}, bf16[4,32,512]{2,1,0:T(8,128)(2,1)S(1)}, u32[]{:S(2)}, u32[]{:S(2)}) collective-permute-start(bf16[4,32,512]{2,1,0:T(8,128)(2,1)} %get-tuple-element.12), channel_id=1, source_target_pairs={{0,64},{32,96},{1,65},{33,97},{2,66},{34,98},{3,67},{35,99},{4,68}... | collective-permute-start | bytes 393224 | tf_op jit(solution)/shard_map/ppermute | solution.py:199
  19.3 2.2 %collective-permute-start.1 = (bf16[4,32,512]{2,1,0:T(8,128)(2,1)}, bf16[4,32,512]{2,1,0:T(8,128)(2,1)S(1)}, u32[]{:S(2)}, u32[]{:S(2)}) collective-permute-start(bf16[4,32,512]{2,1,0:T(8,128)(2,1)} %get-tuple-element.13), channel_id=1, source_target_pairs={{0,128},{32,160},{1,129},{33,161},{2,130},{34,162},{3,131},{35,163... | collective-permute-start | bytes 393224 | tf_op jit(solution)/shard_map/ppermute | solution.py:199
  21.5 1.3 %collective-permute-start.2 = (bf16[4,32,512]{2,1,0:T(8,128)(2,1)}, bf16[4,32,512]{2,1,0:T(8,128)(2,1)S(1)}, u32[]{:S(2)}, u32[]{:S(2)}) collective-permute-start(bf16[4,32,512]{2,1,0:T(8,128)(2,1)} %get-tuple-element.14), channel_id=1, source_target_pairs={{0,192},{32,224},{1,193},{33,225},{2,194},{34,226},{3,195},{35,227... | collective-permute-start | bytes 393224 | tf_op jit(solution)/shard_map/ppermute | solution.py:199
  22.8 1.7 %collective-permute-done.far_a = bf16[4,32,512]{2,1,0:T(8,128)(2,1)S(1)} collective-permute-done((bf16[4,32,512]{2,1,0:T(8,128)(2,1)}, bf16[4,32,512]{2,1,0:T(8,128)(2,1)S(1)}, u32[]{:S(2)}, u32[]{:S(2)}) %collective-permute-start) | collective-permute-done | bytes 131104 | tf_op jit(solution)/shard_map/ppermute | solution.py:199
  24.6 5.6 %collective-permute-done.1.far_b = bf16[4,32,512]{2,1,0:T(8,128)(2,1)S(1)} collective-permute-done((bf16[4,32,512]{2,1,0:T(8,128)(2,1)}, bf16[4,32,512]{2,1,0:T(8,128)(2,1)S(1)}, u32[]{:S(2)}, u32[]{:S(2)}) %collective-permute-start.1) | collective-permute-done | bytes 131104 | tf_op jit(solution)/shard_map/ppermute | solution.py:199
  30.2 1.2 %shard_map.75 = (bf16[4,32,512]{2,1,0:T(8,128)(2,1)S(1)}, bf16[4,32,512]{2,1,0:T(8,128)(2,1)S(1)}) custom-call(s32[4,8]{1,0:T(4,128)S(1)} %bitcast.16, s32[4,2,8]{2,1,0:T(2,128)S(1)} %bitcast.18, f32[8,128]{1,0:T(8,128)S(1)} %bitcast.20, bf16[8,25,16,128]{3,2,1,0:T(8,128)(2,1)S(1)} %all-to-all-done.tiles.got, f32[512,512]{1,0:T(8,128)S(1)} %copy-done, ...), custom_call_target="tpu_custom_call" | custom-call | flops 1000000 | bytes 2000000 | tf_op jit(solution)/shard_map/pallas_call | solution.py:200
  31.5 12.8 %collective-permute-start.8 = (bf16[4,32,512]{2,1,0:T(8,128)(2,1)S(1)}, bf16[4,32,512]{2,1,0:T(8,128)(2,1)S(1)}, u32[]{:S(2)}, u32[]{:S(2)}) collective-permute-start(bf16[4,32,512]{2,1,0:T(8,128)(2,1)S(1)} %get-tuple-element.16), channel_id=1, source_target_pairs={{0,16},{1,48},{2,80},{3,112},{4,144},{5,176},{6,208},{7,240},{32,2... | collective-permute-start | bytes 393224 | tf_op jit(solution)/shard_map/ppermute | solution.py:212
  44.3 1.3 %collective-permute-start.7 = (bf16[4,32,512]{2,1,0:T(8,128)(2,1)S(1)}, bf16[4,32,512]{2,1,0:T(8,128)(2,1)S(1)}, u32[]{:S(2)}, u32[]{:S(2)}) collective-permute-start(bf16[4,32,512]{2,1,0:T(8,128)(2,1)S(1)} %get-tuple-element.16), channel_id=1, source_target_pairs={{0,0},{1,32},{2,64},{3,96},{4,128},{5,160},{6,192},{7,224},{32,5},... | collective-permute-start | bytes 393224 | tf_op jit(solution)/shard_map/ppermute | solution.py:212
  45.6 3.5 %collective-permute-start.3 = (bf16[4,32,512]{2,1,0:T(8,128)(2,1)S(1)}, bf16[4,32,512]{2,1,0:T(8,128)(2,1)S(1)}, u32[]{:S(2)}, u32[]{:S(2)}) collective-permute-start(bf16[4,32,512]{2,1,0:T(8,128)(2,1)S(1)} %get-tuple-element.15), channel_id=1, source_target_pairs={{0,32},{32,0},{64,96},{96,64},{128,160},{160,128},{192,224},{224,1... | collective-permute-start | bytes 393224 | tf_op jit(solution)/shard_map/ppermute | solution.py:221
  49.1 1.3 %shard_map.74.base = f32[512,512]{1,0:T(8,128)S(1)} custom-call(s32[4,8]{1,0:T(4,128)S(1)} %bitcast.17, s32[4,2,8]{2,1,0:T(2,128)S(1)} %bitcast.19, f32[512,512]{1,0:T(8,128)S(1)} %copy-done, bf16[8,25,16,128]{3,2,1,0:T(8,128)(2,1)S(1)} %all-to-all-done.tiles.got), custom_call_target="tpu_custom_call" | custom-call | flops 1000000 | bytes 3000000 | tf_op jit(solution)/shard_map/pallas_call | solution.py:231
  50.5 0.7 collective-permute-start.10
  51.2 0.7 collective-permute-start.11
  51.9 1.3 %collective-permute-start.9 = (bf16[2,4,32,512]{3,2,1,0:T(8,128)(2,1)S(1)}, bf16[2,4,32,512]{3,2,1,0:T(8,128)(2,1)S(1)}, u32[]{:S(2)}, u32[]{:S(2)}) collective-permute-start(bf16[2,4,32,512]{3,2,1,0:T(8,128)(2,1)S(1)} %pad_maximum_fusion.1), channel_id=1, source_target_pairs={{0,4},{5,1},{10,14},{15,11},{16,20},{21,17},{26,30},{31,27},{32,36... | collective-permute-start | bytes 786440 | tf_op jit(solution)/shard_map/ppermute | solution.py:215
  53.4 2.1 %collective-permute-start.5 = (bf16[2,4,32,512]{3,2,1,0:T(8,128)(2,1)S(1)}, bf16[2,4,32,512]{3,2,1,0:T(8,128)(2,1)S(1)}, u32[]{:S(2)}, u32[]{:S(2)}) collective-permute-start(bf16[2,4,32,512]{3,2,1,0:T(8,128)(2,1)S(1)} %pad_maximum_fusion), channel_id=1, source_target_pairs={{0,128},{32,160},{64,192},{96,224},{128,0},{160,32},{192,64},{224,... | collective-permute-start | bytes 786440 | tf_op jit(solution)/shard_map/ppermute | solution.py:221
  55.5 1.7 %collective-permute-start.6 = (bf16[2,4,32,512]{3,2,1,0:T(8,128)(2,1)S(1)}, bf16[2,4,32,512]{3,2,1,0:T(8,128)(2,1)S(1)}, u32[]{:S(2)}, u32[]{:S(2)}) collective-permute-start(bf16[2,4,32,512]{3,2,1,0:T(8,128)(2,1)S(1)} %pad_maximum_fusion), channel_id=1, source_target_pairs={{0,192},{32,224},{64,128},{96,160},{128,64},{160,96},{192,0},{224,... | collective-permute-start | bytes 786440 | tf_op jit(solution)/shard_map/ppermute | solution.py:221
  57.2 8.8 %collective-permute-done.9 = bf16[2,4,32,512]{3,2,1,0:T(8,128)(2,1)S(1)} collective-permute-done((bf16[2,4,32,512]{3,2,1,0:T(8,128)(2,1)S(1)}, bf16[2,4,32,512]{3,2,1,0:T(8,128)(2,1)S(1)}, u32[]{:S(2)}, u32[]{:S(2)}) %collective-permute-start.9) | collective-permute-done | bytes 262176 | tf_op jit(solution)/shard_map/ppermute | solution.py:215
  66.2 0.7 collective-permute-start.12
  66.9 7.4 %collective-permute-done.13.left_c = bf16[2,4,32,512]{3,2,1,0:T(8,128)(2,1)S(1)} collective-permute-done((bf16[2,4,32,512]{3,2,1,0:T(8,128)(2,1)S(1)}, bf16[2,4,32,512]{3,2,1,0:T(8,128)(2,1)S(1)}, u32[]{:S(2)}, u32[]{:S(2)}) %collective-permute-start.13) | collective-permute-done | bytes 262176 | tf_op jit(solution)/shard_map/ppermute | solution.py:218
  74.2 0.6 collective-permute-start.14
  74.9 0.6 shard_map.76.so_far
  75.5 0.5 collective-permute-done.14.left
  76.0 1.2 %shard_map.77 = f32[512,512]{1,0:T(8,128)} custom-call(f32[512,512]{1,0:T(8,128)S(1)} %shard_map.76.so_far, bf16[8,4,32,512]{3,2,1,0:T(8,128)(2,1)S(1)} %constant_dynamic-update-slice_fusion.got.panel, bf16[2,4,32,512]{3,2,1,0:T(8,128)(2,1)S(1)} %collective-permute-done.14.left), custom_call_target="tpu_custom_call" | custom-call | flops 135000000 | bytes 3000000 | tf_op jit(solution)/shard_map/pallas_call | solution.py:236
  (29 shorter events, 0.4 us)
Async XLA Ops:
  0.0 30.2 %copy-start.1 = (s32[8,4,1]{0,2,1:T(1,128)S(1)}, s32[8,4,1]{0,2,1:T(1,128)}, u32[]{:S(2)}) copy-start(s32[8,4,1]{0,2,1:T(1,128)} %param.10) | copy-start | bytes 388
  0.0 30.2 %copy-start = (f32[512,512]{1,0:T(8,128)S(1)}, f32[512,512]{1,0:T(8,128)}, u32[]{:S(2)}) copy-start(f32[512,512]{1,0:T(8,128)} %slab.3) | copy-start | bytes 3145732
  0.0 30.2 %copy-start.2 = (s32[8,4,2]{0,2,1:T(2,128)S(1)}, s32[8,4,2]{0,2,1:T(2,128)}, u32[]{:S(2)}) copy-start(s32[8,4,2]{0,2,1:T(2,128)} %param.11) | copy-start | bytes 772
  0.0 30.2 %copy-start.3 = (f32[1024]{0:T(1024)S(1)}, f32[1024]{0:T(1024)}, u32[]{:S(2)}) copy-start(f32[1024]{0:T(1024)} %param.13) | copy-start | bytes 12292
  8.5 21.7 %all-to-all-start = ((bf16[8,25,16,128]{3,2,1,0:T(8,128)(2,1)}), bf16[8,25,16,128]{3,2,1,0:T(8,128)(2,1)S(1)}, u32[]{:S(2)}, u32[]{:S(2)}) async-start(bf16[8,25,16,128]{3,2,1,0:T(8,128)(2,1)} %bitcast.23), calls=%async_computation | async-start | bytes 1638400 | tf_op jit(solution)/shard_map/all_to_all | solution.py:198
  16.0 8.6 %collective-permute-start = (bf16[4,32,512]{2,1,0:T(8,128)(2,1)}, bf16[4,32,512]{2,1,0:T(8,128)(2,1)S(1)}, u32[]{:S(2)}, u32[]{:S(2)}) collective-permute-start(bf16[4,32,512]{2,1,0:T(8,128)(2,1)} %get-tuple-element.12), channel_id=1, source_target_pairs={{0,64},{32,96},{1,65},{33,97},{2,66},{34,98},{3,67},{35,99},{4,68}... | collective-permute-start | bytes 393224 | tf_op jit(solution)/shard_map/ppermute | solution.py:199
  19.3 10.9 %collective-permute-start.1 = (bf16[4,32,512]{2,1,0:T(8,128)(2,1)}, bf16[4,32,512]{2,1,0:T(8,128)(2,1)S(1)}, u32[]{:S(2)}, u32[]{:S(2)}) collective-permute-start(bf16[4,32,512]{2,1,0:T(8,128)(2,1)} %get-tuple-element.13), channel_id=1, source_target_pairs={{0,128},{32,160},{1,129},{33,161},{2,130},{34,162},{3,131},{35,163... | collective-permute-start | bytes 393224 | tf_op jit(solution)/shard_map/ppermute | solution.py:199
  21.5 8.7 %collective-permute-start.2 = (bf16[4,32,512]{2,1,0:T(8,128)(2,1)}, bf16[4,32,512]{2,1,0:T(8,128)(2,1)S(1)}, u32[]{:S(2)}, u32[]{:S(2)}) collective-permute-start(bf16[4,32,512]{2,1,0:T(8,128)(2,1)} %get-tuple-element.14), channel_id=1, source_target_pairs={{0,192},{32,224},{1,193},{33,225},{2,194},{34,226},{3,195},{35,227... | collective-permute-start | bytes 393224 | tf_op jit(solution)/shard_map/ppermute | solution.py:199
  31.5 19.0 %collective-permute-start.8 = (bf16[4,32,512]{2,1,0:T(8,128)(2,1)S(1)}, bf16[4,32,512]{2,1,0:T(8,128)(2,1)S(1)}, u32[]{:S(2)}, u32[]{:S(2)}) collective-permute-start(bf16[4,32,512]{2,1,0:T(8,128)(2,1)S(1)} %get-tuple-element.16), channel_id=1, source_target_pairs={{0,16},{1,48},{2,80},{3,112},{4,144},{5,176},{6,208},{7,240},{32,2... | collective-permute-start | bytes 393224 | tf_op jit(solution)/shard_map/ppermute | solution.py:212
  44.3 6.2 %collective-permute-start.7 = (bf16[4,32,512]{2,1,0:T(8,128)(2,1)S(1)}, bf16[4,32,512]{2,1,0:T(8,128)(2,1)S(1)}, u32[]{:S(2)}, u32[]{:S(2)}) collective-permute-start(bf16[4,32,512]{2,1,0:T(8,128)(2,1)S(1)} %get-tuple-element.16), channel_id=1, source_target_pairs={{0,0},{1,32},{2,64},{3,96},{4,128},{5,160},{6,192},{7,224},{32,5},... | collective-permute-start | bytes 393224 | tf_op jit(solution)/shard_map/ppermute | solution.py:212
  45.6 7.6 %collective-permute-start.3 = (bf16[4,32,512]{2,1,0:T(8,128)(2,1)S(1)}, bf16[4,32,512]{2,1,0:T(8,128)(2,1)S(1)}, u32[]{:S(2)}, u32[]{:S(2)}) collective-permute-start(bf16[4,32,512]{2,1,0:T(8,128)(2,1)S(1)} %get-tuple-element.15), channel_id=1, source_target_pairs={{0,32},{32,0},{64,96},{96,64},{128,160},{160,128},{192,224},{224,1... | collective-permute-start | bytes 393224 | tf_op jit(solution)/shard_map/ppermute | solution.py:221
  50.5 5.0 %collective-permute-start.10 = (bf16[2,4,32,512]{3,2,1,0:T(8,128)(2,1)S(1)}, bf16[2,4,32,512]{3,2,1,0:T(8,128)(2,1)S(1)}, u32[]{:S(2)}, u32[]{:S(2)}) collective-permute-start(bf16[2,4,32,512]{3,2,1,0:T(8,128)(2,1)S(1)} %pad_maximum_fusion.1), channel_id=1, source_target_pairs={{0,8},{5,13},{10,2},{15,7},{16,24},{21,29},{26,18},{31,23},{32,40}... | collective-permute-start | bytes 786440 | tf_op jit(solution)/shard_map/ppermute | solution.py:215
  51.2 6.0 %collective-permute-start.11 = (bf16[2,4,32,512]{3,2,1,0:T(8,128)(2,1)S(1)}, bf16[2,4,32,512]{3,2,1,0:T(8,128)(2,1)S(1)}, u32[]{:S(2)}, u32[]{:S(2)}) collective-permute-start(bf16[2,4,32,512]{3,2,1,0:T(8,128)(2,1)S(1)} %pad_maximum_fusion.1), channel_id=1, source_target_pairs={{0,12},{5,9},{10,6},{15,3},{16,28},{21,25},{26,22},{31,19},{32,44}... | collective-permute-start | bytes 786440 | tf_op jit(solution)/shard_map/ppermute | solution.py:215
  51.9 14.1 %collective-permute-start.9 = (bf16[2,4,32,512]{3,2,1,0:T(8,128)(2,1)S(1)}, bf16[2,4,32,512]{3,2,1,0:T(8,128)(2,1)S(1)}, u32[]{:S(2)}, u32[]{:S(2)}) collective-permute-start(bf16[2,4,32,512]{3,2,1,0:T(8,128)(2,1)S(1)} %pad_maximum_fusion.1), channel_id=1, source_target_pairs={{0,4},{5,1},{10,14},{15,11},{16,20},{21,17},{26,30},{31,27},{32,36... | collective-permute-start | bytes 786440 | tf_op jit(solution)/shard_map/ppermute | solution.py:215
  53.3 13.6 %collective-permute-start.4 = (bf16[2,4,32,512]{3,2,1,0:T(8,128)(2,1)S(1)}, bf16[2,4,32,512]{3,2,1,0:T(8,128)(2,1)S(1)}, u32[]{:S(2)}, u32[]{:S(2)}) collective-permute-start(bf16[2,4,32,512]{3,2,1,0:T(8,128)(2,1)S(1)} %pad_maximum_fusion), channel_id=1, source_target_pairs={{0,64},{32,96},{64,0},{96,32},{128,192},{160,224},{192,128},{224,1... | collective-permute-start | bytes 786440 | tf_op jit(solution)/shard_map/ppermute | solution.py:221
  53.4 21.5 %collective-permute-start.5 = (bf16[2,4,32,512]{3,2,1,0:T(8,128)(2,1)S(1)}, bf16[2,4,32,512]{3,2,1,0:T(8,128)(2,1)S(1)}, u32[]{:S(2)}, u32[]{:S(2)}) collective-permute-start(bf16[2,4,32,512]{3,2,1,0:T(8,128)(2,1)S(1)} %pad_maximum_fusion), channel_id=1, source_target_pairs={{0,128},{32,160},{64,192},{96,224},{128,0},{160,32},{192,64},{224,... | collective-permute-start | bytes 786440 | tf_op jit(solution)/shard_map/ppermute | solution.py:221
  55.5 19.4 %collective-permute-start.6 = (bf16[2,4,32,512]{3,2,1,0:T(8,128)(2,1)S(1)}, bf16[2,4,32,512]{3,2,1,0:T(8,128)(2,1)S(1)}, u32[]{:S(2)}, u32[]{:S(2)}) collective-permute-start(bf16[2,4,32,512]{3,2,1,0:T(8,128)(2,1)S(1)} %pad_maximum_fusion), channel_id=1, source_target_pairs={{0,192},{32,224},{64,128},{96,160},{128,64},{160,96},{192,0},{224,... | collective-permute-start | bytes 786440 | tf_op jit(solution)/shard_map/ppermute | solution.py:221
  66.1 8.2 %collective-permute-start.13 = (bf16[2,4,32,512]{3,2,1,0:T(8,128)(2,1)S(1)}, bf16[2,4,32,512]{3,2,1,0:T(8,128)(2,1)S(1)}, u32[]{:S(2)}, u32[]{:S(2)}) collective-permute-start(bf16[2,4,32,512]{3,2,1,0:T(8,128)(2,1)S(1)} %add_add_fusion.left_a), channel_id=1, source_target_pairs={{0,2},{1,3},{2,0},{3,1},{4,6},{5,7},{6,4},{7,5},{8,10},{9,11},{10,... | collective-permute-start | bytes 786440 | tf_op jit(solution)/shard_map/ppermute | solution.py:218
  66.2 8.8 %collective-permute-start.12 = (bf16[2,4,32,512]{3,2,1,0:T(8,128)(2,1)S(1)}, bf16[2,4,32,512]{3,2,1,0:T(8,128)(2,1)S(1)}, u32[]{:S(2)}, u32[]{:S(2)}) collective-permute-start(bf16[2,4,32,512]{3,2,1,0:T(8,128)(2,1)S(1)} %add_add_fusion.left_a), channel_id=1, source_target_pairs={{0,1},{1,0},{2,3},{3,2},{4,5},{5,4},{6,7},{7,6},{8,9},{9,8},{10,11... | collective-permute-start | bytes 786440 | tf_op jit(solution)/shard_map/ppermute | solution.py:218
  74.2 1.8 %collective-permute-start.14 = (bf16[2,4,32,512]{3,2,1,0:T(8,128)(2,1)S(1)}, bf16[2,4,32,512]{3,2,1,0:T(8,128)(2,1)S(1)}, u32[]{:S(2)}, u32[]{:S(2)}) collective-permute-start(bf16[2,4,32,512]{3,2,1,0:T(8,128)(2,1)S(1)} %collective-permute-done.13.left_c), channel_id=1, source_target_pairs={{0,1},{1,0},{2,3},{3,2},{4,5},{5,4},{6,7},{7,6},{8,9},{9,8},{10,11... | collective-permute-start | bytes 786440 | tf_op jit(solution)/shard_map/ppermute | solution.py:218
